TPU v7x, 256 devices: a whole 4x4x8 slice. The times are simulated.
256 devices in a mesh: rep: 8 (over z_hi, x), fsdp: 32 (over y, z_lo, core).
Axes of the slice: x: 4, y: 4, z: 8 (z_hi: 2, z_lo: 4; z = z_hi * 4 + z_lo), core: 2. Of those that a mesh axis runs over, the one named last changes fastest.
Arguments:
- images: bfloat16 [256, 16, 32, 320], P(('rep', 'fsdp')), may hold values from -6 to 6
- w_down: bfloat16 [2880, 320], P('fsdp'), may hold values from -0.109375 to 0.109375
- w_conv: bfloat16 [2880, 640], P('fsdp'), may hold values from -0.109375 to 0.109375
- w_skip: bfloat16 [320, 640], P('fsdp'), may hold values from -0.3125 to 0.3125
- act_grad: bfloat16 [256, 8, 16, 640], P(('rep', 'fsdp')), may hold values from -6 to 6
- short_grad: bfloat16 [256, 8, 16, 640], P(('rep', 'fsdp')), may hold values from -6 to 6
Outputs:
- activated: bfloat16 [256, 8, 16, 640], P(('rep', 'fsdp'))
- shortcut: bfloat16 [256, 8, 16, 640], P(('rep', 'fsdp'))
- grad_down: float32 [2880, 320], P('fsdp')
- grad_conv: float32 [2880, 640], P('fsdp')
- grad_skip: float32 [320, 640], P('fsdp')
All inputs are finite; a program needn't handle non-finite values.
Results may differ from a plain program's by a relative error of at most 0.029.
Values may be sent and summed in bfloat16 or wider, within the bound.
A program may use at most 128 MiB of HBM per device.

v0:
```python
import jax
import jax.numpy as jnp
from jax import lax
from jax.sharding import PartitionSpec as P

GROUPS = 32


def as_sent(shard):
    return jax.tree.map(lambda a: a.astype(jnp.bfloat16) if a.dtype == jnp.float32 else a, shard)


def norm_silu(values):
    grouped = values.reshape(
        values.shape[0], values.shape[1] * values.shape[2], GROUPS, values.shape[3] // GROUPS
    )
    average = jnp.mean(grouped, axis=(1, 3), keepdims=True)
    centred = grouped - average
    spread = jnp.mean(centred * centred, axis=(1, 3), keepdims=True)
    normed = centred * lax.rsqrt(spread + 1e-05)
    return jax.nn.silu(normed).reshape(values.shape)


def convolve(inputs, weight, stride):
    kernel = weight.reshape(3, 3, inputs.shape[3], weight.shape[1])
    return lax.conv_general_dilated(
        inputs,
        kernel,
        (stride, stride),
        ((1, 1), (1, 1)),
        dimension_numbers=("NHWC", "HWIO", "NHWC"),
        preferred_element_type=jnp.float32,
    )


def forward(pictures, w_down, w_conv, w_skip):
    reduced = convolve(pictures, w_down, 2).astype(jnp.bfloat16)
    first = norm_silu(reduced.astype(jnp.float32)).astype(jnp.bfloat16)
    hidden = convolve(first, w_conv, 1).astype(jnp.bfloat16)
    activated = norm_silu(hidden.astype(jnp.float32)).astype(jnp.bfloat16)
    shortcut = jnp.dot(reduced, w_skip, preferred_element_type=jnp.float32).astype(jnp.bfloat16)
    return (activated, shortcut)


def body(images, w_down, w_conv, w_skip, act_grad, short_grad):
    gathered = (
        lax.all_gather(w_down, "fsdp", axis=0, tiled=True),
        lax.all_gather(w_conv, "fsdp", axis=0, tiled=True),
        lax.all_gather(w_skip, "fsdp", axis=0, tiled=True),
    )
    activated, shortcut = forward(images, gathered[0], gathered[1], gathered[2])
    backward_kernels = (
        lax.all_gather(w_down, "fsdp", axis=0, tiled=True),
        lax.all_gather(w_conv, "fsdp", axis=0, tiled=True),
        lax.all_gather(w_skip, "fsdp", axis=0, tiled=True),
    )

    def local_forward(kernel_down, kernel_conv, kernel_skip):
        return forward(images, kernel_down, kernel_conv, kernel_skip)

    unused, pullback = jax.vjp(
        local_forward, backward_kernels[0], backward_kernels[1], backward_kernels[2]
    )
    gradients = pullback((act_grad, short_grad))
    replicas = lax.axis_size("rep")
    shard_count = lax.axis_size("fsdp")
    inverse = 1.0 / (replicas * shard_count * images.shape[0])
    partials = tuple((grad.astype(jnp.float32) for grad in gradients))
    shards = jax.tree.map(
        lambda part: part.astype(jnp.float32),
        lax.psum_scatter(as_sent(partials), "fsdp", scatter_dimension=0, tiled=True),
    )
    summed = lax.psum(shards, "rep")
    return (activated, shortcut, summed[0] * inverse, summed[1] * inverse, summed[2] * inverse)


def solution(mesh):
    placed = (
        P(("rep", "fsdp"), None, None, None),
        P("fsdp", None),
        P("fsdp", None),
        P("fsdp", None),
        P(("rep", "fsdp"), None, None, None),
        P(("rep", "fsdp"), None, None, None),
    )
    return jax.shard_map(
        body,
        mesh=mesh,
        in_specs=placed,
        out_specs=(
            P(("rep", "fsdp"), None, None, None),
            P(("rep", "fsdp"), None, None, None),
            P("fsdp", None),
            P("fsdp", None),
            P("fsdp", None),
        ),
        check_vma=False,
    )
```

profile of v0, /device:TPU:8, one launch (start us, length us, event | category | flops | bytes accessed | tf_op | source)
XLA Modules:
  0.0 582.1 jit_solution(305875304420563648)
XLA Ops:
  8.7 1.1 copy.89
  10.9 40.5 %all-gather.2 = bf16[32,10,640]{2,1,0:T(8,128)(2,1)S(1)} all-gather(bf16[1,10,640]{2,1,0:T(8,128)(2,1)} %bitcast.136), channel_id=1, replica_groups=mesh['rep'=8,'fsdp'=32] {'fsdp'}, dimensions={0}, use_global_device_ids=true | all-gather | bytes 422400 | tf_op jit(solution)/shard_map/all_gather | solution.py:49
  53.4 20.2 %all-gather.6.cloned.1.call-done = bf16[32,90,320]{2,1,0:T(8,128)(2,1)} async-done(((bf16[1,90,320]{2,1,0:T(8,128)(2,1)}), bf16[32,90,320]{2,1,0:T(8,128)(2,1)}) %all-gather.6.cloned.1.call-update) | async-done | bytes 1843216 | tf_op jit(solution)/shard_map/all_gather | solution.py:47
  73.7 2.9 reshape.286
  76.6 1.7 select_reduce_fusion.4
  79.5 0.9 fusion.8
  81.2 1.1 fusion.3
  83.3 53.9 %all-gather.8.cloned.1.call-done = bf16[32,90,640]{2,1,0:T(8,128)(2,1)} async-done(((bf16[1,90,640]{2,1,0:T(8,128)(2,1)}), bf16[32,90,640]{2,1,0:T(8,128)(2,1)}) %all-gather.8.cloned.1.call-update) | async-done | bytes 3686416 | tf_op jit(solution)/shard_map/all_gather | solution.py:48
  137.2 4.9 reshape.287
  142.1 3.1 select_reduce_fusion.1
  148.3 3.7 select_reduce_fusion.2
  153.5 3.6 convolution_convert_fusion.1
  157.1 3.3 convolution_convert_fusion
  160.4 81.9 %fusion.62 = (bf16[96,320]{1,0:T(8,128)(2,1)S(1)}, bf16[96,640]{1,0:T(8,128)(2,1)S(1)}) fusion(bf16[2880,320]{1,0:T(8,128)(2,1)S(1)} %bitcast.122, bf16[2880,640]{1,0:T(8,128)(2,1)} %bitcast.118), kind=kCustom, calls=%all-reduce-scatter.2 | all-reduce-scatter fusion | flops 2949121 | bytes 5714944
  242.3 1.9 collective-permute-start
  244.3 1.9 collective-permute-start.1
  246.2 149.9 %all-reduce.10.cloned.1.call-done = bf16[320,640]{1,0:T(8,128)(2,1)} async-done(((bf16[320,640]{1,0:T(8,128)(2,1)}), bf16[320,640]{1,0:T(8,128)(2,1)}) %all-reduce.10.cloned.1.call-update) | async-done | bytes 409616
  396.8 1.9 collective-permute-start.2
  398.8 52.4 %psum.23 = f32[10,640]{1,0:T(8,128)S(1)} all-reduce(f32[10,640]{1,0:T(8,128)S(1)} %dynamic-slice_convert_fusion.2), channel_id=1, replica_groups=mesh['rep'=8,'fsdp'=32] {'rep'}, use_global_device_ids=true, to_apply=%region_21.22 | all-reduce | flops 6400 | bytes 51200 | tf_op jit(solution)/shard_map/psum | solution.py:73
  451.2 1.9 collective-permute-start.3
  454.6 6.1 %collective-permute-done.3 = bf16[90,640]{1,0:T(8,128)(2,1)S(1)} collective-permute-done((bf16[90,640]{1,0:T(8,128)(2,1)S(1)}, bf16[90,640]{1,0:T(8,128)(2,1)S(1)}, u32[]{:S(2)}, u32[]{:S(2)}) %collective-permute-start.3) | collective-permute-done | bytes 115232
  463.6 108.8 %all-reduce.12.cloned.1.call-done = (f32[90,320]{1,0:T(8,128)}, f32[90,640]{1,0:T(8,128)}) async-done(((f32[90,320]{1,0:T(8,128)}, f32[90,640]{1,0:T(8,128)}), (f32[90,320]{1,0:T(8,128)}, f32[90,640]{1,0:T(8,128)})) %all-reduce.12.cloned.1.call-update) | async-done | bytes 345616 | tf_op jit(solution)/shard_map/psum | solution.py:73
  572.3 1.6 broadcast_multiply_fusion.3
  573.9 1.7 broadcast_multiply_fusion.2
  (112 shorter events, 15.6 us)
Async XLA Ops:
  7.2 74.1 %copy-start = (bf16[1,8,16,640]{3,2,1,0:T(8,128)(2,1)S(1)}, bf16[1,8,16,640]{3,2,1,0:T(8,128)(2,1)}, u32[]{:S(2)}) copy-start(bf16[1,8,16,640]{3,2,1,0:T(8,128)(2,1)} %param.11) | copy-start | bytes 491524
  7.2 44.4 %copy-start.6 = (u32[256]{0:T(256)S(1)}, u32[256]{0:T(256)}, u32[]{:S(2)}) copy-start(u32[256]{0:T(256)} %constant.71) | copy-start | bytes 3076
  7.2 66.5 %all-gather.6.cloned.1.call-start = ((), (), s32[]{:S(2)}) async-start(), calls=%async_computation | async-start | bytes 2433024 | tf_op jit(solution)/shard_map/all_gather | solution.py:47
  7.9 129.3 %all-gather.8.cloned.1.call-start = ((), (), s32[]{:S(2)}) async-start(), calls=%async_computation.1 | async-start | bytes 4055040 | tf_op jit(solution)/shard_map/all_gather | solution.py:48
  8.7 387.4 %all-reduce.10.cloned.1.call-start = ((), (), s32[]{:S(2)}) async-start(), calls=%async_computation.2 | async-start | bytes 819200
  9.9 66.7 %copy-start.5 = (pred[8,3]{0,1:T(4,128)(4,1)S(1)}, pred[8,3]{0,1:T(4,128)(4,1)}, u32[]{:S(2)}) copy-start(pred[8,3]{0,1:T(4,128)(4,1)} %constant.59) | copy-start | bytes 76
  82.3 490.0 %all-reduce.12.cloned.1.call-start = ((), (), s32[]{:S(2)}) async-start(), calls=%async_computation.3 | async-start | bytes 786432 | tf_op jit(solution)/shard_map/psum | solution.py:73
  145.6 1.3 copy-start.1
  153.5 3.6 copy-start.2
  153.5 3.6 copy-start.3
  153.5 3.6 copy-start.4
  242.3 210.8 %collective-permute-start = (bf16[96,320]{1,0:T(8,128)(2,1)S(1)}, bf16[96,320]{1,0:T(8,128)(2,1)S(1)}, u32[]{:S(2)}, u32[]{:S(2)}) collective-permute-start(bf16[96,320]{1,0:T(8,128)(2,1)S(1)} %get-tuple-element.19), channel_id=1, source_target_pairs={{0,1},{1,2},{2,3},{3,4},{4,5},{5,6},{6,7},{7,8},{8,9},{9,10},{10,1... | collective-permute-start | bytes 184328
  244.3 208.9 %collective-permute-start.1 = (bf16[90,320]{1,0:T(8,128)(2,1)S(1)}, bf16[90,320]{1,0:T(8,128)(2,1)S(1)}, u32[]{:S(2)}, u32[]{:S(2)}) collective-permute-start(bf16[90,320]{1,0:T(8,128)(2,1)S(1)} %slice.32), channel_id=1, source_target_pairs={{0,2},{1,3},{2,4},{3,5},{4,6},{5,7},{6,8},{7,9},{8,10},{9,11},{10,... | collective-permute-start | bytes 172808
  396.8 63.8 %collective-permute-start.2 = (bf16[96,640]{1,0:T(8,128)(2,1)S(1)}, bf16[96,640]{1,0:T(8,128)(2,1)S(1)}, u32[]{:S(2)}, u32[]{:S(2)}) collective-permute-start(bf16[96,640]{1,0:T(8,128)(2,1)S(1)} %get-tuple-element.20), channel_id=1, source_target_pairs={{0,1},{1,2},{2,3},{3,4},{4,5},{5,6},{6,7},{7,8},{8,9},{9,10},{10,1... | collective-permute-start | bytes 368648
  451.2 9.5 %collective-permute-start.3 = (bf16[90,640]{1,0:T(8,128)(2,1)S(1)}, bf16[90,640]{1,0:T(8,128)(2,1)S(1)}, u32[]{:S(2)}, u32[]{:S(2)}) collective-permute-start(bf16[90,640]{1,0:T(8,128)(2,1)S(1)} %slice.33), channel_id=1, source_target_pairs={{0,2},{1,3},{2,4},{3,5},{4,6},{5,7},{6,8},{7,9},{8,10},{9,11},{10,... | collective-permute-start | bytes 345608
Sparse Core Ops, SparseCore 0:
  9.9 63.7 all-gather.5
  75.5 61.6 all-gather.7
  139.9 256.1 all-reduce.9
  462.3 109.9 all-reduce.11
where the time goes:
time: 583 us; the launch traced here: 582 us
  waiting for transfers between devices  340 us (58%)
  blocking collectives  175 us (30%)
  matrix products  17.6 us (3%)
  local copies, waits for them, and re-layouts  16 us (3%)
  between operations  15.7 us (3%)
  other arithmetic  9.67 us (2%)
  starting transfers between devices  8.01 us (1%)
    unnamed x9, waiting for transfers between devices  157 us
    psum x1, waiting for transfers between devices, body(): summed = lax.psum(shards, 'rep')  109 us
    unnamed x1, blocking collectives  81.9 us
    all_gather x1, waiting for transfers between devices, body(): lax.all_gather(w_conv, 'fsdp', axis=0, tiled=True)  53.9 us
    psum x1, blocking collectives, body(): summed = lax.psum(shards, 'rep')  52.4 us
    all_gather x1, blocking collectives, body(): lax.all_gather(w_skip, 'fsdp', axis=0, tiled=True)  40.5 us
    all_gather x1, waiting for transfers between devices, body(): lax.all_gather(w_down, 'fsdp', axis=0, tiled=True)  20.2 us
    conv_general_dilated x5, matrix products, convolve(): lax.conv_general_dilated(inputs, kernel, (stride, stride), ((1, 1), (1, 1...  15.3 us
  transfers between devices with their start and end apart: 8, of which 5 were waited for; matrix products, arithmetic and copies ran while one was open for 21% of the time, Pallas kernels for 0%

commit v1 on v0

v1 whole, which is shorter than its diff:
```python
import jax
import jax.numpy as jnp
from jax import lax
from jax.experimental import pallas as pl
from jax.experimental.pallas import tpu as pltpu
from jax.sharding import PartitionSpec as P

MESH = pl.DeviceIdType.MESH
BF = jnp.bfloat16
F32 = jnp.float32

C0, C1 = 320, 640
LANES0 = 384
SHARD = 90
PAD = 96
SKIP, SKIP_PAD = 10, 16
ROWS_A, ROWS_B = PAD, PAD + SKIP_PAD
HALF_A, HALF_B = 48, 64
PART = 32
CELLS = 128
TILE = 256
COLS = 32 * PAD
CHUNK = 8 * PAD
SEMS = 160
EPS = 1e-5


def source_of(col):
    shard, place = divmod(col, PAD)
    return SHARD * shard + place if place < SHARD else -1


def tile_taps():
    pairs = []
    for tile in range(COLS // TILE):
        cols = [source_of(c) for c in range(tile * TILE, (tile + 1) * TILE)]
        for tap in sorted({s // C0 for s in cols if s >= 0}):
            pairs.append((tile, tap))
    return pairs


PAIRS = tile_taps()


def iota(shape, axis):
    return lax.broadcasted_iota(jnp.int32, shape, axis)


def ones_where(mask):
    return jnp.where(mask, 1.0, 0.0).astype(BF)


def spread_matrix(tile, tap):
    lane = iota((1, TILE), 1) + tile * TILE
    shard = jnp.full((1, TILE), tile * TILE // PAD, jnp.int32)
    for edge in range(PAD, COLS, PAD):
        if tile * TILE < edge < (tile + 1) * TILE:
            shard = shard + jnp.where(lane >= edge, 1, 0)
    place = lane - PAD * shard
    channel = lane - (PAD - SHARD) * shard - C0 * tap
    good = (place < SHARD) & (channel >= 0) & (channel < C0)
    channel = jnp.where(good, channel, -1)
    return ones_where(iota((LANES0, TILE), 0) == channel)


def skip_matrix():
    lane = iota((1, 32 * SKIP_PAD), 1)
    shard = lane >> 4
    place = lane - SKIP_PAD * shard
    channel = jnp.where(place < SKIP, SKIP * shard + place, -1)
    return ones_where(iota((LANES0, 32 * SKIP_PAD), 0) == channel)


def shift_down(tap):
    kh, kw = divmod(tap, 3)
    cell = iota((CELLS, 1), 0)
    row, col = 2 * (cell >> 4) + kh - 1, 2 * (cell & 15) + kw - 1
    index = jnp.where((row >= 0) & (col >= 0), row * 32 + col, -1)
    return ones_where(iota((CELLS, 512), 1) == index)


def shift_conv(tap):
    kh, kw = divmod(tap, 3)
    cell = iota((CELLS, 1), 0)
    row, col = (cell >> 4) + kh - 1, (cell & 15) + kw - 1
    good = (row >= 0) & (row < 8) & (col >= 0) & (col < 16)
    index = jnp.where(good, row * 16 + col, -1)
    return ones_where(iota((CELLS, CELLS), 1) == index)


def dot(a, b):
    return lax.dot_general(a, b, (((1,), (0,)), ((), ())), preferred_element_type=F32)


def dot_nt(a, b):
    return lax.dot_general(a, b, (((1,), (1,)), ((), ())), preferred_element_type=F32)


def dot_tn(a, b):
    return lax.dot_general(a, b, (((0,), (0,)), ((), ())), preferred_element_type=F32)


def group_matrix(width, group_of):
    return ones_where(group_of(iota((width, width), 0)) == group_of(iota((width, width), 1)))


def group10(c):
    return (c * 6554) >> 16


def group20(c):
    return (c * 3277) >> 16


def group_sums(vectors, same):
    width = same.shape[0]
    row = iota((8, width), 0)
    stacked = jnp.zeros((8, width), F32)
    for number, vector in enumerate(vectors):
        rest = vector
        for term in range(3):
            part = rest.astype(BF).astype(F32)
            rest = rest - part
            stacked = jnp.where(row == 4 * number + term, part, stacked)
    sums = dot(stacked.astype(BF), same)
    return [jnp.sum(sums[4 * n : 4 * n + 4], axis=0, keepdims=True) for n in range(len(vectors))]


def normalise(values, same, count):
    (total,) = group_sums([jnp.sum(values, axis=0, keepdims=True)], same)
    centred = values - total * (1.0 / count)
    (square,) = group_sums([jnp.sum(centred * centred, axis=0, keepdims=True)], same)
    scale = lax.rsqrt(square * (1.0 / count) + EPS)
    return centred * scale, scale


def normalise_back(cotangent, normed, scale, same, count):
    sig = 1.0 / (1.0 + jnp.exp(-normed))
    slope = cotangent * (sig * (1.0 + normed * (1.0 - sig)))
    first, second = group_sums(
        [jnp.sum(slope, axis=0, keepdims=True), jnp.sum(slope * normed, axis=0, keepdims=True)], same
    )
    return scale * (slope - first * (1.0 / count) - normed * (second * (1.0 / count)))


def silu(normed):
    return normed / (1.0 + jnp.exp(-normed))


class Copies:
    def __init__(self, send, recv):
        self.send, self.recv, self.started = send, recv, []

    def start(self, src, dst, device):
        number = len(self.started)
        copy = pltpu.make_async_remote_copy(
            src_ref=src,
            dst_ref=dst,
            send_sem=self.send.at[number],
            recv_sem=self.recv.at[number],
            device_id=device,
            device_id_type=MESH,
        )
        copy.start()
        self.started.append(copy)
        return copy


class Gather:
    def __init__(self, copies, piece, place, after, before):
        self.copies, self.piece, self.place = copies, piece, place
        self.after, self.before = after, before

    def send(self, chunk, half, device):
        ref = self.piece(chunk, half)
        return self.copies.start(ref, ref, device)

    def start(self):
        self.first = self.send(self.place, None, self.after)
        self.second = self.send(self.place, None, self.before)

    def forward(self):
        self.first.wait_recv()
        self.third = self.send((self.place + 3) % 4, 0, self.after)
        self.second.wait_recv()
        self.fourth = self.send((self.place + 1) % 4, 1, self.before)

    def finish(self):
        self.third.wait_recv()
        self.fourth.wait_recv()


def add_into(ref, *others):
    total = ref[...].astype(F32)
    for other in others:
        total = total + other[...].astype(F32)
    ref[...] = total.astype(BF)


class Scatter:
    def __init__(self, copies, piece, place, after, before, lands):
        self.copies, self.piece, self.place = copies, piece, place
        self.after, self.before, self.lands = after, before, lands

    def send(self, chunk, half, slot, device):
        return self.copies.start(self.piece(chunk % 4, half), self.lands[half].at[slot], device)

    def start(self):
        p = self.place
        self.c0 = self.send(p + 2, 0, 0, self.after)
        self.c1 = self.send(p + 2, 1, 0, self.before)
        self.c2 = self.send(p + 1, 1, 1, self.after)
        self.c3 = self.send(p + 3, 0, 1, self.before)

    def middle(self):
        p = self.place
        self.c0.wait_recv()
        add_into(self.piece((p + 1) % 4, 0), self.lands[0].at[0])
        self.c4 = self.send(p + 1, 0, 2, self.after)
        self.c1.wait_recv()
        add_into(self.piece((p + 3) % 4, 1), self.lands[1].at[0])
        self.c5 = self.send(p + 3, 1, 2, self.before)

    def finish(self):
        self.c2.wait_recv()
        self.c3.wait_recv()
        self.c4.wait_recv()
        add_into(self.piece(self.place, 0), self.lands[0].at[1], self.lands[0].at[2])
        self.c5.wait_recv()
        add_into(self.piece(self.place, 1), self.lands[1].at[1], self.lands[1].at[2])


def kernel(
    img, wd, wc, ws, ag, sg,
    act_out, short_out, down_out, conv_out, skip_out,
    ga, gb, grad_a, grad_b, sib_a, sib_b, sum_a, sum_b,
    a0y, a1z, a0z0, a0z1, a1y0, a1y1,
    b0y, b1z, b0z0, b0z1, b1y0, b1y1,
    share, share_in, share_z, full,
    spread, padded_img, taps, cols_img, cols_first,
    send, recv,
):
    rep, shard = lax.axis_index("rep"), lax.axis_index("fsdp")
    x, y, zl, core = rep % 4, shard // 8, (shard // 2) % 4, shard % 2
    z = (rep // 4) * 4 + zl

    def device(x, y, z, core):
        return ((z // 4) * 4 + x, (y * 4 + z % 4) * 2 + core)

    sibling = device(x, y, z, 1 - core)
    y_next, y_prev = device(x, (y + 1) % 4, z, core), device(x, (y + 3) % 4, z, core)
    z_next, z_prev = device(x, y, (z + 1) % 8, core), device(x, y, (z + 7) % 8, core)
    z_far = device(x, y, (z + 4) % 8, core)
    x_others = [device((x + d) % 4, y, z, core) for d in (1, 2, 3)]

    ga[y, zl, core] = jnp.zeros((ROWS_A, LANES0), BF)
    ga[y, zl, core, 0:SHARD, 0:C0] = wd[...]
    gb[y, zl, core] = jnp.zeros((ROWS_B, C1), BF)
    gb[y, zl, core, 0:SHARD] = wc[...]
    gb[y, zl, core, PAD : PAD + SKIP] = ws[...]

    barrier = pltpu.get_barrier_semaphore()
    greeted = [sibling, y_next, y_prev, z_next, z_prev, z_far] + x_others
    for other in greeted:
        pl.semaphore_signal(barrier, inc=1, device_id=other, device_id_type=MESH)
    pl.semaphore_wait(barrier, len(greeted))

    copies = Copies(send, recv)

    some = {None: pl.ds(0, 4), 0: pl.ds(0, 2), 1: pl.ds(2, 2)}

    def rows_of(half, low, high):
        return {None: pl.ds(low, high - low), 0: pl.ds(low, PART), 1: pl.ds(low + PART, high - low - PART)}[half]

    def gather_of(buf, rows, half_rows):
        low, high = (0, half_rows), (half_rows, rows)
        one0 = Gather(copies, lambda c, h: buf.at[y, c, core, rows_of(h, *low)], zl, z_next, z_prev)
        one1 = Gather(copies, lambda c, h: buf.at[c, zl, core, rows_of(h, *high)], y, y_next, y_prev)
        two0 = Gather(copies, lambda c, h: buf.at[c, some[h], core, rows_of(None, *low)], y, y_next, y_prev)
        two1 = Gather(copies, lambda c, h: buf.at[some[h], c, core, rows_of(None, *high)], zl, z_next, z_prev)
        return (one0, one1), (two0, two1)

    one_a, two_a = gather_of(ga, ROWS_A, HALF_A)
    one_b, two_b = gather_of(gb, ROWS_B, HALF_B)
    to_sibling = {"a": [], "b": []}

    def share_with_sibling(name, ring, offset):
        ref = ring.piece((ring.place + offset) % 4, None)
        to_sibling[name].append(copies.start(ref, ref, sibling))

    for ring in one_a + one_b:
        ring.start()

    for number, (tile, tap) in enumerate(PAIRS):
        spread[number] = spread_matrix(tile, tap)
    padded_img[...] = jnp.zeros((512, LANES0), BF)
    padded_img[:, 0:C0] = img[...]

    for ring in one_a + one_b:
        ring.forward()

    def columns(out):
        for tile in range(COLS // TILE):
            total = None
            for number, (tile_of, tap) in enumerate(PAIRS):
                if tile_of == tile:
                    term = dot(taps[tap], spread[number])
                    total = term if total is None else total + term
            out[:, tile * TILE : (tile + 1) * TILE] = total.astype(BF)

    for ring in one_a:
        ring.finish()
    for ring in two_a:
        ring.start()
    for ring in two_a:
        share_with_sibling("a", ring, 0)
    for ring in one_b:
        ring.finish()
    for ring in two_b:
        ring.start()
    for ring in two_b:
        share_with_sibling("b", ring, 0)

    for tap in range(9):
        taps[tap] = dot(shift_down(tap), padded_img[...]).astype(BF)

    for ring in two_a:
        ring.forward()
    for ring in two_a:
        share_with_sibling("a", ring, 1)
        share_with_sibling("a", ring, 3)

    columns(cols_img)

    for ring in two_a:
        ring.finish()
        share_with_sibling("a", ring, 2)
    for ring in two_b:
        ring.forward()
    for ring in two_b:
        share_with_sibling("b", ring, 1)
        share_with_sibling("b", ring, 3)
    for copy in to_sibling["a"]:
        copy.wait_recv()

    def chunk_of(q):
        return slice(q * CHUNK, (q + 1) * CHUNK)

    def down_rows(q):
        return ga[q].reshape(CHUNK, LANES0)

    def conv_rows(q):
        return gb[q, :, :, 0:PAD, :].reshape(CHUNK, C1)

    reduced = sum(dot(cols_img[:, chunk_of(q)], down_rows(q)) for q in range(4)).astype(BF)
    same0 = group_matrix(LANES0, group10)
    normed0, scale0 = normalise(reduced.astype(F32), same0, CELLS * (C0 // 32))
    first = silu(normed0).astype(BF)
    for tap in range(9):
        taps[tap] = dot(shift_conv(tap), first).astype(BF)
    columns(cols_first)
    skip_spread = skip_matrix()
    reduced_cols = dot(reduced, skip_spread).astype(BF)
    grad_b[:, :, :, PAD:ROWS_B, :] = dot_tn(reduced_cols, sg[...]).astype(BF).reshape(4, 4, 2, SKIP_PAD, C1)

    for ring in two_b:
        ring.finish()
        share_with_sibling("b", ring, 2)
    for copy in to_sibling["b"]:
        copy.wait_recv()

    hidden = sum(dot(cols_first[:, chunk_of(q)], conv_rows(q)) for q in range(4)).astype(BF)
    same1 = group_matrix(C1, group20)
    normed1, scale1 = normalise(hidden.astype(F32), same1, CELLS * (C1 // 32))
    act_out[...] = silu(normed1).astype(BF)
    d_hidden = normalise_back(ag[...].astype(F32), normed1, scale1, same1, CELLS * (C1 // 32)).astype(BF)

    from_sibling = {"a": [], "b": []}

    def to_other_core(name, grads, lands, q):
        from_sibling[name].append(copies.start(grads.at[q, :, 1 - core], lands.at[q], sibling))

    def add_cores(name, grads, lands, sums):
        for q in range(4):
            from_sibling[name][q].wait_recv()
            sums[q] = (grads[q, :, core].astype(F32) + lands[q].astype(F32)).astype(BF)

    for q in range(4):
        part = dot_tn(cols_first[:, chunk_of(q)], d_hidden).astype(BF)
        grad_b[q, :, :, 0:PAD, :] = part.reshape(4, 2, PAD, C1)
        to_other_core("b", grad_b, sib_b, q)

    def scatter_of(buf, rows, half_rows, lands0y, lands1z, lands0z, lands1y):
        low, high = (0, half_rows), (half_rows, rows)
        one0 = Scatter(copies, lambda c, h: buf.at[c, some[h], rows_of(None, *low)], y, y_next, y_prev,
                       (lands0y.at[0], lands0y.at[1]))
        one1 = Scatter(copies, lambda c, h: buf.at[some[h], c, rows_of(None, *high)], zl, z_next, z_prev,
                       (lands1z.at[0], lands1z.at[1]))
        two0 = Scatter(copies, lambda c, h: buf.at[y, c, rows_of(h, *low)], zl, z_next, z_prev, lands0z)
        two1 = Scatter(copies, lambda c, h: buf.at[c, zl, rows_of(h, *high)], y, y_next, y_prev, lands1y)
        return (one0, one1), (two0, two1)

    down_a, down2_a = scatter_of(sum_a, ROWS_A, HALF_A, a0y, a1z, (a0z0, a0z1), (a1y0, a1y1))
    down_b, down2_b = scatter_of(sum_b, ROWS_B, HALF_B, b0y, b1z, (b0z0, b0z1), (b1y0, b1y1))

    for q in range(4):
        cols_first[:, chunk_of(q)] = dot_nt(d_hidden, conv_rows(q)).astype(BF)

    add_cores("b", grad_b, sib_b, sum_b)
    for ring in down_b:
        ring.start()

    d_first = jnp.zeros((CELLS, LANES0), F32)
    for tap in range(9):
        part = None
        for number, (tile, tap_of) in enumerate(PAIRS):
            if tap_of == tap:
                term = dot_nt(cols_first[:, tile * TILE : (tile + 1) * TILE], spread[number])
                part = term if part is None else part + term
        d_first = d_first + dot(shift_conv(8 - tap), part.astype(BF))

    skip_rows = gb[:, :, :, PAD:ROWS_B, :].reshape(32 * SKIP_PAD, C1)
    short_out[...] = dot(reduced_cols, skip_rows).astype(BF)
    d_skip = dot_nt(dot_nt(sg[...], skip_rows).astype(BF), skip_spread)
    d_norm = normalise_back(
        d_first.astype(BF).astype(F32), normed0, scale0, same0, CELLS * (C0 // 32)
    )
    d_reduced = (d_norm + d_skip).astype(BF)

    for q in range(4):
        part = dot_tn(cols_img[:, chunk_of(q)], d_reduced).astype(BF)
        grad_a[q] = part.reshape(4, 2, PAD, LANES0)
        to_other_core("a", grad_a, sib_a, q)

    for ring in down_b:
        ring.middle()
    add_cores("a", grad_a, sib_a, sum_a)
    for ring in down_a:
        ring.start()
    for ring in down_b:
        ring.finish()
    for ring in down2_b:
        ring.start()
    for ring in down_a:
        ring.middle()
    for ring in down2_b:
        ring.middle()
    for ring in down_a:
        ring.finish()
    for ring in down2_a:
        ring.start()
    for ring in down2_b:
        ring.finish()
    for ring in down2_a:
        ring.middle()
    for ring in down2_a:
        ring.finish()

    for tile in range(5):
        share[tile] = sum_b[y, zl, :, tile * 128 : (tile + 1) * 128]
    for tile in range(3):
        share[5 + tile] = jnp.zeros((ROWS_B, 128), BF)
        share[5 + tile, 0:PAD] = sum_a[y, zl, :, tile * 128 : (tile + 1) * 128]
    spread_out = [
        copies.start(share.at[pl.ds(2 * ((x + d) % 4), 2)], share_in.at[d - 1], x_others[d - 1])
        for d in (1, 2, 3)
    ]
    for copy in spread_out:
        copy.wait_recv()
    total = share[pl.ds(2 * x, 2)].astype(F32)
    for slot in range(3):
        total = total + share_in[slot].astype(F32)
    share_z[0] = total.astype(BF)
    copy = copies.start(share_z.at[0], share_z.at[1], z_far)
    copy.wait_recv()
    full[pl.ds(2 * x, 2)] = (share_z[0].astype(F32) + share_z[1].astype(F32)).astype(BF)
    mine = full.at[pl.ds(2 * x, 2)]
    gathered = [copies.start(mine, mine, other) for other in x_others]
    for copy in gathered:
        copy.wait_recv()

    inverse = 1.0 / 256
    for tile in range(5):
        lanes = slice(tile * 128, (tile + 1) * 128)
        values = full[tile].astype(F32) * inverse
        conv_out[:, lanes] = values[0:SHARD]
        skip_out[:, lanes] = values[PAD : PAD + SKIP]
    for tile in range(3):
        high = min(C0, (tile + 1) * 128)
        values = full[5 + tile].astype(F32) * inverse
        down_out[:, tile * 128 : high] = values[0:SHARD, 0 : high - tile * 128]

    for copy in copies.started:
        copy.wait_send()


def vmem(*shape):
    return pltpu.VMEM(shape, BF)


def body(images, w_down, w_conv, w_skip, act_grad, short_grad):
    picture = images.reshape(512, C0)
    act_cot = act_grad.reshape(CELLS, C1)
    short_cot = short_grad.reshape(CELLS, C1)

    def lands(lanes, low, high):
        return [
            vmem(2, 3, 2, low, lanes),
            vmem(2, 3, 2, high, lanes),
            vmem(3, PART, lanes),
            vmem(3, low - PART, lanes),
            vmem(3, PART, lanes),
            vmem(3, high - PART, lanes),
        ]

    outs = pl.pallas_call(
        kernel,
        out_shape=(
            jax.ShapeDtypeStruct((CELLS, C1), BF),
            jax.ShapeDtypeStruct((CELLS, C1), BF),
            jax.ShapeDtypeStruct((SHARD, C0), F32),
            jax.ShapeDtypeStruct((SHARD, C1), F32),
            jax.ShapeDtypeStruct((SKIP, C1), F32),
        ),
        in_specs=[pl.BlockSpec(memory_space=pltpu.VMEM)] * 6,
        out_specs=tuple([pl.BlockSpec(memory_space=pltpu.VMEM)] * 5),
        scratch_shapes=[
            vmem(4, 4, 2, ROWS_A, LANES0),
            vmem(4, 4, 2, ROWS_B, C1),
            vmem(4, 4, 2, ROWS_A, LANES0),
            vmem(4, 4, 2, ROWS_B, C1),
            vmem(4, 4, ROWS_A, LANES0),
            vmem(4, 4, ROWS_B, C1),
            vmem(4, 4, ROWS_A, LANES0),
            vmem(4, 4, ROWS_B, C1),
            *lands(LANES0, HALF_A, ROWS_A - HALF_A),
            *lands(C1, HALF_B, ROWS_B - HALF_B),
            vmem(8, ROWS_B, 128),
            vmem(3, 2, ROWS_B, 128),
            vmem(2, 2, ROWS_B, 128),
            vmem(8, ROWS_B, 128),
            vmem(len(PAIRS), LANES0, TILE),
            vmem(512, LANES0),
            vmem(9, CELLS, LANES0),
            vmem(CELLS, COLS),
            vmem(CELLS, COLS),
            pltpu.SemaphoreType.DMA((SEMS,)),
            pltpu.SemaphoreType.DMA((SEMS,)),
        ],
        compiler_params=pltpu.CompilerParams(
            collective_id=0, has_side_effects=True, vmem_limit_bytes=56 * 1024 * 1024
        ),
    )(picture, w_down, w_conv, w_skip, act_cot, short_cot)
    activated, shortcut, down, conv, skip = outs
    return (
        activated.reshape(act_grad.shape),
        shortcut.reshape(short_grad.shape),
        down,
        conv,
        skip,
    )


def solution(mesh):
    cells = P(("rep", "fsdp"), None, None, None)
    rows = P("fsdp", None)
    return jax.shard_map(
        body,
        mesh=mesh,
        in_specs=(cells, rows, rows, rows, cells, cells),
        out_specs=(cells, cells, rows, rows, rows),
        check_vma=False,
    )
```

time: 583 us -> 94.7 us (0.16)
  waiting for transfers between devices: 340 us -> 0 us
  blocking collectives: 175 us -> 0 us
  Pallas kernels: 0 us -> 89.2 us
  matrix products: 17.6 us -> 0 us
  between operations: 15.7 us -> 0.66 us
  local copies, waits for them, and re-layouts: 16 us -> 4.38 us
  other arithmetic: 9.67 us -> 0 us
  starting transfers between devices: 8.01 us -> 0 us
    unnamed x9 -> x0, waiting for transfers between devices: 157 us -> none
    psum x1 -> x0, waiting for transfers between devices: 109 us -> none  [body(): summed = lax.psum(shards, 'rep')]
    pallas_call x0 -> x1, Pallas kernels: none -> 89.2 us  [body(): pl.pallas_call(kernel, out_shape=(jax.ShapeDtypeStruct((CELLS, C1), BF),...]
    unnamed x1 -> x0, blocking collectives: 81.9 us -> none
    all_gather x2 -> x0, waiting for transfers between devices: 74.1 us -> none  [the longest x1 53.9 us: body(): lax.all_gather(w_conv, 'fsdp', axis=0, tiled=True)]
    psum x1 -> x0, blocking collectives: 52.4 us -> none  [body(): summed = lax.psum(shards, 'rep')]
    all_gather x1 -> x0, blocking collectives: 40.5 us -> none  [body(): lax.all_gather(w_skip, 'fsdp', axis=0, tiled=True)]
    conv_general_dilated x5 -> x0, matrix products: 15.3 us -> none  [convolve(): lax.conv_general_dilated(inputs, kernel, (stride, stride), ((1, 1), (1, 1...]
  transfers between devices with their start and end apart: 8 -> 0, of which waited for: 5 -> 0; matrix products, arithmetic and copies ran while one was open for 21% -> 0% of each run, Pallas kernels for 0% -> 0%
where the time goes in v1:
time: 94.7 us; the launch traced here: 94.3 us
  Pallas kernels  89.2 us (94%)
  local copies, waits for them, and re-layouts  4.38 us (5%)
    pallas_call x1, Pallas kernels, body(): pl.pallas_call(kernel, out_shape=(jax.ShapeDtypeStruct((CELLS, C1), BF),...  89.2 us
    unnamed x13, local copies, waits for them, and re-layouts  4.38 us

profile of v1, /device:TPU:8, one launch (start us, length us, event | category | flops | bytes accessed | tf_op | source)
XLA Modules:
  0.0 94.3 jit_solution(17010268294897177683)
XLA Ops:
  0.6 89.2 %shard_map.101 = (bf16[128,640]{1,0:T(8,128)(2,1)}, bf16[128,640]{1,0:T(8,128)(2,1)}, f32[90,320]{1,0:T(8,128)}, f32[90,640]{1,0:T(8,128)}, f32[10,640]{1,0:T(8,128)}) custom-call(bf16[512,320]{1,0:T(8,128)(2,1)} %bitcast.5, bf16[90,320]{1,0:T(8,128)(2,1)} %wd.1, bf16[90,640]{1,0:T(8,128)(2,1)} %wc.1, bf16[10,640]{1,0:T(8,128)(2,1)} %ws.1, ...), custom_call_target="tpu_custom_call" | custom-call | tf_op jit(solution)/shard_map/pallas_call | solution.py:516
  89.9 0.0 copy-start.1
  89.9 0.0 copy-start.2
  89.9 1.6 %copy.16 = bf16[1,8,16,640]{3,2,1,0:T(8,128)(2,1)} copy(bf16[1,8,16,640]{3,2,1,0:T(8,128)(2,1)} %bitcast.9) | data formatting | bytes 327680
  91.5 0.0 copy-done.1
  91.5 0.0 copy-start
  91.5 0.7 copy.17
  92.2 0.0 copy-done.2
  92.2 0.7 copy.18
  92.9 0.0 copy-done
  92.9 0.0 copy-start.3
  92.9 0.7 copy.19
  93.6 0.1 copy-done.3
  93.7 0.6 copy.20
Async XLA Ops:
  89.9 1.7 %copy-start.1 = (bf16[128,640]{1,0:T(8,128)(2,1)S(1)}, bf16[128,640]{1,0:T(8,128)(2,1)}, u32[]{:S(2)}) copy-start(bf16[128,640]{1,0:T(8,128)(2,1)} %get-tuple-element.11) | copy-start | bytes 491524
  89.9 2.3 %copy-start.2 = (f32[90,320]{1,0:T(8,128)S(1)}, f32[90,320]{1,0:T(8,128)}, u32[]{:S(2)}) copy-start(f32[90,320]{1,0:T(8,128)} %get-tuple-element.22) | copy-start | bytes 345604
  91.5 1.3 %copy-start = (f32[90,640]{1,0:T(8,128)S(1)}, f32[90,640]{1,0:T(8,128)}, u32[]{:S(2)}) copy-start(f32[90,640]{1,0:T(8,128)} %get-tuple-element.23) | copy-start | bytes 691204
  92.9 0.8 copy-start.3

commit v2 on v1

v2 whole, which is shorter than its diff:
```python
import jax
import jax.numpy as jnp
from jax import lax
from jax.experimental import pallas as pl
from jax.experimental.pallas import tpu as pltpu
from jax.sharding import PartitionSpec as P

MESH = pl.DeviceIdType.MESH
BF = jnp.bfloat16
F32 = jnp.float32

C0, C1 = 320, 640
LANES0 = 384
SHARD = 90
PAD = 96
SKIP, SKIP_PAD = 10, 16
ROW_TILES = PAD // 16
CELLS = 128
TILE = 256
COLS = 32 * PAD
CHUNK = 8 * PAD
SEMS = 240
EPS = 1e-5


def source_of(col):
    shard, place = divmod(col, PAD)
    return SHARD * shard + place if place < SHARD else -1


def tile_taps():
    pairs = []
    for tile in range(COLS // TILE):
        cols = [source_of(c) for c in range(tile * TILE, (tile + 1) * TILE)]
        for tap in sorted({s // C0 for s in cols if s >= 0}):
            pairs.append((tile, tap))
    return pairs


PAIRS = tile_taps()


def iota(shape, axis):
    return lax.broadcasted_iota(jnp.int32, shape, axis)


def ones_where(mask):
    return jnp.where(mask, 1.0, 0.0).astype(BF)


def spread_matrix(tile, tap):
    lane = iota((1, TILE), 1) + tile * TILE
    shard = jnp.full((1, TILE), tile * TILE // PAD, jnp.int32)
    for edge in range(PAD, COLS, PAD):
        if tile * TILE < edge < (tile + 1) * TILE:
            shard = shard + jnp.where(lane >= edge, 1, 0)
    place = lane - PAD * shard
    channel = lane - (PAD - SHARD) * shard - C0 * tap
    good = (place < SHARD) & (channel >= 0) & (channel < C0)
    channel = jnp.where(good, channel, -1)
    return ones_where(iota((LANES0, TILE), 0) == channel)


def skip_matrix():
    lane = iota((1, 32 * SKIP_PAD), 1)
    shard = lane >> 4
    place = lane - SKIP_PAD * shard
    channel = jnp.where(place < SKIP, SKIP * shard + place, -1)
    return ones_where(iota((LANES0, 32 * SKIP_PAD), 0) == channel)


def shift_down(tap):
    kh, kw = divmod(tap, 3)
    cell = iota((CELLS, 1), 0)
    row, col = 2 * (cell >> 4) + kh - 1, 2 * (cell & 15) + kw - 1
    index = jnp.where((row >= 0) & (col >= 0), row * 32 + col, -1)
    return ones_where(iota((CELLS, 512), 1) == index)


def shift_conv(tap):
    kh, kw = divmod(tap, 3)
    cell = iota((CELLS, 1), 0)
    row, col = (cell >> 4) + kh - 1, (cell & 15) + kw - 1
    good = (row >= 0) & (row < 8) & (col >= 0) & (col < 16)
    index = jnp.where(good, row * 16 + col, -1)
    return ones_where(iota((CELLS, CELLS), 1) == index)


def dot(a, b):
    return lax.dot_general(a, b, (((1,), (0,)), ((), ())), preferred_element_type=F32)


def dot_nt(a, b):
    return lax.dot_general(a, b, (((1,), (1,)), ((), ())), preferred_element_type=F32)


def dot_tn(a, b):
    return lax.dot_general(a, b, (((0,), (0,)), ((), ())), preferred_element_type=F32)


def group_matrix(width, group_of):
    return ones_where(group_of(iota((width, width), 0)) == group_of(iota((width, width), 1)))


def group10(c):
    return (c * 6554) >> 16


def group20(c):
    return (c * 3277) >> 16


def group_sums(vectors, same):
    width = same.shape[0]
    row = iota((8, width), 0)
    stacked = jnp.zeros((8, width), F32)
    for number, vector in enumerate(vectors):
        rest = vector
        for term in range(3):
            part = rest.astype(BF).astype(F32)
            rest = rest - part
            stacked = jnp.where(row == 4 * number + term, part, stacked)
    sums = dot(stacked.astype(BF), same)
    return [jnp.sum(sums[4 * n : 4 * n + 4], axis=0, keepdims=True) for n in range(len(vectors))]


def normalise(values, same, count):
    (total,) = group_sums([jnp.sum(values, axis=0, keepdims=True)], same)
    centred = values - total * (1.0 / count)
    (square,) = group_sums([jnp.sum(centred * centred, axis=0, keepdims=True)], same)
    scale = lax.rsqrt(square * (1.0 / count) + EPS)
    return centred * scale, scale


def normalise_back(cotangent, normed, scale, same, count):
    sig = 1.0 / (1.0 + jnp.exp(-normed))
    slope = cotangent * (sig * (1.0 + normed * (1.0 - sig)))
    first, second = group_sums(
        [jnp.sum(slope, axis=0, keepdims=True), jnp.sum(slope * normed, axis=0, keepdims=True)], same
    )
    return scale * (slope - first * (1.0 / count) - normed * (second * (1.0 / count)))


def silu(normed):
    return normed / (1.0 + jnp.exp(-normed))


class Tiles:
    def __init__(self, quarter, middle, end, slots):
        self.quarter, self.middle, self.end, self.slots = quarter, middle, end, slots
        self.from1 = 4 * quarter
        self.from2 = self.from1 + middle
        self.count1, self.count2 = middle, end
        self.rest = (slots - self.from1) // 4
        self.own = quarter + self.rest

    def place(self, tile):
        if tile < self.from1:
            return tile // self.quarter, tile % self.quarter
        tile -= self.from1
        return tile // self.rest, self.quarter + tile % self.rest


TILES_A = Tiles(2, 4, 6, 20)
TILES_B = Tiles(4, 12, 7, 36)

ALL, LOW, HIGH = pl.ds(0, 4), pl.ds(0, 2), pl.ds(2, 2)
SOME = {None: ALL, 0: LOW, 1: HIGH}


def part_of(start, count, half):
    first = (count + 1) // 2
    if half is None:
        return pl.ds(start, count)
    return pl.ds(start, first) if half == 0 else pl.ds(start + first, count - first)


def part_size(count, half):
    return (count + 1) // 2 if half == 0 else count // 2


class Copies:
    def __init__(self, send, recv):
        self.send, self.recv, self.started = send, recv, []

    def start(self, src, dst, device):
        number = len(self.started)
        copy = pltpu.make_async_remote_copy(
            src_ref=src,
            dst_ref=dst,
            send_sem=self.send.at[number],
            recv_sem=self.recv.at[number],
            device_id=device,
            device_id_type=MESH,
        )
        copy.start()
        self.started.append(copy)
        return copy


class Gather:
    def __init__(self, copies, piece, ring):
        self.copies, self.piece = copies, piece
        self.place, self.after, self.before = ring

    def send(self, chunk, half, device):
        ref = self.piece(chunk, half)
        return self.copies.start(ref, ref, device)

    def start(self):
        self.first = self.send(self.place, None, self.after)
        self.second = self.send(self.place, None, self.before)

    def forward(self):
        self.first.wait_recv()
        self.third = self.send((self.place + 3) % 4, 0, self.after)
        self.second.wait_recv()
        self.fourth = self.send((self.place + 1) % 4, 1, self.before)

    def finish(self):
        self.third.wait_recv()
        self.fourth.wait_recv()


def add_into(ref, *others):
    total = ref[...].astype(F32)
    for other in others:
        total = total + other[...].astype(F32)
    ref[...] = total.astype(BF)


class Scatter:
    def __init__(self, copies, piece, ring, lands):
        self.copies, self.piece = copies, piece
        self.place, self.after, self.before = ring
        self.lands = lands

    def send(self, chunk, half, slot, device):
        return self.copies.start(self.piece(chunk % 4, half), self.lands[half].at[slot], device)

    def start(self):
        p = self.place
        self.c0 = self.send(p + 2, 0, 0, self.after)
        self.c1 = self.send(p + 2, 1, 0, self.before)
        self.c2 = self.send(p + 1, 1, 1, self.after)
        self.c3 = self.send(p + 3, 0, 1, self.before)

    def middle(self):
        p = self.place
        self.c0.wait_recv()
        add_into(self.piece((p + 1) % 4, 0), self.lands[0].at[0])
        self.c4 = self.send(p + 1, 0, 2, self.after)
        self.c1.wait_recv()
        add_into(self.piece((p + 3) % 4, 1), self.lands[1].at[0])
        self.c5 = self.send(p + 3, 1, 2, self.before)

    def finish(self):
        self.c2.wait_recv()
        self.c3.wait_recv()
        self.c4.wait_recv()
        add_into(self.piece(self.place, 0), self.lands[0].at[1], self.lands[0].at[2])
        self.c5.wait_recv()
        add_into(self.piece(self.place, 1), self.lands[1].at[1], self.lands[1].at[2])


def scatter_slots(cut):
    shapes = []
    for shape in ((2, 4, cut.quarter), (2, cut.count1), (2, cut.count2), (2, cut.quarter)):
        shapes.append([shape] * 2)
    for size in (cut.count1, cut.count2, cut.quarter, cut.rest):
        shapes.append([(part_size(size, 0),), (part_size(size, 1),)])
    return shapes


def each(method, *rings):
    for ring in rings:
        getattr(ring, method)()


class Weights:
    def __init__(self, copies, buf, cut, at, rings, sibling):
        x, y, zl, core = at
        on_x, on_y, on_z = rings
        mine = cut.quarter * x
        quarter, one, two = cut.quarter, cut.from1, cut.from2
        n1, n2 = cut.count1, cut.count2
        self.copies, self.sibling, self.shared = copies, sibling, []
        self.first = (
            Gather(copies, lambda c, h: buf.at[y, c, core, part_of(mine, quarter, h)], on_z),
            Gather(copies, lambda c, h: buf.at[y, c, core, part_of(one, n1, h)], on_z),
            Gather(copies, lambda c, h: buf.at[c, zl, core, part_of(two, n2, h)], on_y),
        )
        self.second = (
            Gather(copies, lambda c, h: buf.at[c, SOME[h], core, part_of(mine, quarter, None)], on_y),
            Gather(copies, lambda c, h: buf.at[c, SOME[h], core, part_of(one, n1, None)], on_y),
            Gather(copies, lambda c, h: buf.at[SOME[h], c, core, part_of(two, n2, None)], on_z),
        )
        self.third = Gather(copies, lambda c, h: buf.at[SOME[h], ALL, core, part_of(quarter * c, quarter, None)], on_x)

    def share(self, rings, *offsets):
        for ring in rings:
            for offset in offsets:
                ref = ring.piece((ring.place + offset) % 4, None)
                self.shared.append(self.copies.start(ref, ref, self.sibling))

    def wait_shared(self):
        for copy in self.shared:
            copy.wait_recv()


class Gradients:
    def __init__(self, copies, grads, lands, sums, slots, ends, cut, at, rings, devices):
        x, y, zl, core = at
        on_x, on_y, on_z = rings
        self.copies, self.grads, self.lands, self.sums, self.cut, self.at = copies, grads, lands, sums, cut, at
        self.own, self.far, self.full = ends
        self.sibling, self.z_far, self.x_others = devices
        self.crossed = []
        mine = cut.quarter * x
        quarter, one, two, rest = cut.quarter, cut.from1, cut.from2, cut.rest
        n1, n2 = cut.count1, cut.count2
        pairs = [slots[2 * i : 2 * i + 2] for i in range(8)]
        self.first = (
            Scatter(copies, lambda c, h: sums.at[SOME[h], ALL, part_of(quarter * c, quarter, None)], on_x, pairs[0]),
            Scatter(copies, lambda c, h: sums.at[c, SOME[h], part_of(one, n1, None)], on_y, pairs[1]),
            Scatter(copies, lambda c, h: sums.at[SOME[h], c, part_of(two, n2, None)], on_z, pairs[2]),
        )
        self.second = (
            Scatter(copies, lambda c, h: sums.at[c, SOME[h], part_of(mine, quarter, None)], on_y, pairs[3]),
            Scatter(copies, lambda c, h: sums.at[y, c, part_of(one, n1, h)], on_z, pairs[4]),
            Scatter(copies, lambda c, h: sums.at[c, zl, part_of(two, n2, h)], on_y, pairs[5]),
        )
        self.third = (
            Scatter(copies, lambda c, h: sums.at[y, c, part_of(mine, quarter, h)], on_z, pairs[6]),
            Scatter(copies, lambda c, h: sums.at[y, zl, part_of(one + rest * c, rest, h)], on_x, pairs[7]),
        )

    def cross(self, q):
        core = self.at[3]
        self.crossed.append(self.copies.start(self.grads.at[q, :, 1 - core], self.lands.at[q], self.sibling))

    def add_cores(self):
        core = self.at[3]
        for q in range(4):
            self.crossed[q].wait_recv()
            total = self.grads[q, :, core].astype(F32) + self.lands[q].astype(F32)
            self.sums[q] = total.astype(BF)

    def send_far(self):
        x, y, zl, _ = self.at
        cut = self.cut
        self.own[0 : cut.quarter] = self.sums[y, zl, pl.ds(cut.quarter * x, cut.quarter)]
        self.own[cut.quarter : cut.own] = self.sums[y, zl, pl.ds(cut.from1 + cut.rest * x, cut.rest)]
        self.far_copy = self.copies.start(self.own, self.far, self.z_far)

    def send_full(self):
        x = self.at[0]
        self.far_copy.wait_recv()
        self.full[x] = (self.own[...].astype(F32) + self.far[...].astype(F32)).astype(BF)
        mine = self.full.at[x]
        self.full_copies = [self.copies.start(mine, mine, other) for other in self.x_others]

    def wait_full(self):
        for copy in self.full_copies:
            copy.wait_recv()

    def tile(self, number):
        return self.full[self.cut.place(number)].astype(F32) * (1.0 / 256)


def kernel(
    img, wd, wc, ws, ag, sg,
    act_out, short_out, down_out, conv_out, skip_out,
    ga, gb, grad_a, grad_b, sib_a, sib_b, sum_a, sum_b,
    own_a, own_b, far_a, far_b, full_a, full_b,
    spread, padded_img, taps, cols_img, cols_first,
    send, recv, *slots,
):
    rep, shard = lax.axis_index("rep"), lax.axis_index("fsdp")
    x, y, zl, core = rep % 4, shard // 8, (shard // 2) % 4, shard % 2
    z = (rep // 4) * 4 + zl

    def device(x, y, z, core):
        return ((z // 4) * 4 + x, (y * 4 + z % 4) * 2 + core)

    sibling = device(x, y, z, 1 - core)
    x_others = [device((x + d) % 4, y, z, core) for d in (1, 2, 3)]
    y_next, y_prev = device(x, (y + 1) % 4, z, core), device(x, (y + 3) % 4, z, core)
    z_next, z_prev = device(x, y, (z + 1) % 8, core), device(x, y, (z + 7) % 8, core)
    z_far = device(x, y, (z + 4) % 8, core)
    at = (x, y, zl, core)
    rings = ((x, x_others[0], x_others[2]), (y, y_next, y_prev), (zl, z_next, z_prev))

    def place_shard(buf, values, lane_tile, per_lane, lanes):
        low = lane_tile * 128
        base = per_lane * lane_tile
        if lanes < 128:
            for row in range(ROW_TILES):
                buf[y, zl, core, base + row] = jnp.zeros((16, 128), BF)
            for row in range(ROW_TILES):
                high = min(SHARD, 16 * row + 16)
                buf[y, zl, core, base + row, 0 : high - 16 * row, 0:lanes] = values[16 * row : high, low : low + lanes]
        else:
            full = values[0:80, low : low + 128].reshape(5, 16, 128)
            buf[y, zl, core, base : base + 5] = full
            buf[y, zl, core, base + 5] = jnp.zeros((16, 128), BF)
            buf[y, zl, core, base + 5, 0:10] = values[80:SHARD, low : low + 128]

    for tile in range(3):
        place_shard(ga, wd, tile, 6, min(128, C0 - 128 * tile))
    for tile in range(5):
        place_shard(gb, wc, tile, 7, 128)
        gb[y, zl, core, 7 * tile + 6] = jnp.zeros((16, 128), BF)
        gb[y, zl, core, 7 * tile + 6, 0:SKIP] = ws[:, 128 * tile : 128 * tile + 128]

    barrier = pltpu.get_barrier_semaphore()
    greeted = [sibling, y_next, y_prev, z_next, z_prev, z_far] + x_others
    for other in greeted:
        pl.semaphore_signal(barrier, inc=1, device_id=other, device_id_type=MESH)
    pl.semaphore_wait(barrier, len(greeted))

    copies = Copies(send, recv)
    wa = Weights(copies, ga, TILES_A, at, rings, sibling)
    wb = Weights(copies, gb, TILES_B, at, rings, sibling)

    each("start", *wa.first)
    each("start", *wb.first)

    for number, (tile, tap) in enumerate(PAIRS):
        spread[number] = spread_matrix(tile, tap)
    padded_img[...] = jnp.zeros((512, LANES0), BF)
    padded_img[:, 0:C0] = img[...]

    each("forward", *wa.first)
    each("finish", *wa.first)
    each("start", *wa.second)
    each("forward", *wb.first)
    each("finish", *wb.first)
    each("start", *wb.second)
    wa.share(wa.second[1:], 0)
    wb.share(wb.second[1:], 0)

    for tap in range(9):
        taps[tap] = dot(shift_down(tap), padded_img[...]).astype(BF)

    def columns(out):
        for tile in range(COLS // TILE):
            total = None
            for number, (tile_of, tap) in enumerate(PAIRS):
                if tile_of == tile:
                    term = dot(taps[tap], spread[number])
                    total = term if total is None else total + term
            out[:, tile * TILE : (tile + 1) * TILE] = total.astype(BF)

    each("forward", *wa.second)
    wa.share(wa.second[1:], 1, 3)
    each("finish", *wa.second)
    wa.third.start()
    wa.share(wa.second[1:], 2)
    wa.share([wa.third], 0)
    each("forward", *wb.second)
    wb.share(wb.second[1:], 1, 3)

    columns(cols_img)

    wa.third.forward()
    wa.share([wa.third], 1, 3)
    each("finish", *wb.second)
    wb.third.start()
    wb.share(wb.second[1:], 2)
    wb.share([wb.third], 0)
    wa.third.finish()
    wa.share([wa.third], 2)
    wa.wait_shared()

    def chunk_of(q):
        return slice(q * CHUNK, (q + 1) * CHUNK)

    def rows_of(buf, q, lane_tiles, per_lane):
        parts = [
            buf[q, :, :, per_lane * tile : per_lane * tile + ROW_TILES].reshape(CHUNK, 128)
            for tile in range(lane_tiles)
        ]
        return jnp.concatenate(parts, axis=1)

    def down_rows(q):
        return rows_of(ga, q, 3, 6)

    def conv_rows(q):
        return rows_of(gb, q, 5, 7)

    reduced = sum(dot(cols_img[:, chunk_of(q)], down_rows(q)) for q in range(4)).astype(BF)
    same0 = group_matrix(LANES0, group10)
    normed0, scale0 = normalise(reduced.astype(F32), same0, CELLS * (C0 // 32))
    first = silu(normed0).astype(BF)
    for tap in range(9):
        taps[tap] = dot(shift_conv(tap), first).astype(BF)
    wb.third.forward()
    wb.share([wb.third], 1, 3)
    columns(cols_first)
    skip_spread = skip_matrix()
    reduced_cols = dot(reduced, skip_spread).astype(BF)
    grad_skip = dot_tn(reduced_cols, sg[...]).astype(BF)
    for tile in range(5):
        grad_b[:, :, :, 7 * tile + 6] = grad_skip[:, 128 * tile : 128 * tile + 128].reshape(4, 4, 2, 16, 128)
    grad_b[:, :, :, 35] = jnp.zeros((4, 4, 2, 16, 128), BF)
    grad_a[:, :, :, 18:20] = jnp.zeros((4, 4, 2, 2, 16, 128), BF)

    wb.third.finish()
    wb.share([wb.third], 2)
    wb.wait_shared()

    hidden = sum(dot(cols_first[:, chunk_of(q)], conv_rows(q)) for q in range(4)).astype(BF)
    same1 = group_matrix(C1, group20)
    normed1, scale1 = normalise(hidden.astype(F32), same1, CELLS * (C1 // 32))
    act_out[...] = silu(normed1).astype(BF)
    d_hidden = normalise_back(ag[...].astype(F32), normed1, scale1, same1, CELLS * (C1 // 32)).astype(BF)

    devices = (sibling, z_far, x_others)
    back_a = Gradients(copies, grad_a, sib_a, sum_a, slots[:16], (own_a, far_a, full_a), TILES_A, at, rings, devices)
    back_b = Gradients(copies, grad_b, sib_b, sum_b, slots[16:], (own_b, far_b, full_b), TILES_B, at, rings, devices)

    for q in range(4):
        part = dot_tn(cols_first[:, chunk_of(q)], d_hidden).astype(BF)
        for tile in range(5):
            grad_b[q, :, :, 7 * tile : 7 * tile + 6] = part[:, 128 * tile : 128 * tile + 128].reshape(4, 2, 6, 16, 128)
        back_b.cross(q)

    for q in range(4):
        cols_first[:, chunk_of(q)] = dot_nt(d_hidden, conv_rows(q)).astype(BF)

    back_b.add_cores()
    each("start", *back_b.first)

    d_first = jnp.zeros((CELLS, LANES0), F32)
    for tap in range(9):
        part = None
        for number, (tile, tap_of) in enumerate(PAIRS):
            if tap_of == tap:
                term = dot_nt(cols_first[:, tile * TILE : (tile + 1) * TILE], spread[number])
                part = term if part is None else part + term
        d_first = d_first + dot(shift_conv(8 - tap), part.astype(BF))

    skip_rows = jnp.concatenate([gb[:, :, :, 7 * tile + 6].reshape(512, 128) for tile in range(5)], axis=1)
    short_out[...] = dot(reduced_cols, skip_rows).astype(BF)
    d_skip = dot_nt(dot_nt(sg[...], skip_rows).astype(BF), skip_spread)
    d_norm = normalise_back(
        d_first.astype(BF).astype(F32), normed0, scale0, same0, CELLS * (C0 // 32)
    )
    d_reduced = (d_norm + d_skip).astype(BF)

    for q in range(4):
        part = dot_tn(cols_img[:, chunk_of(q)], d_reduced).astype(BF)
        for tile in range(3):
            grad_a[q, :, :, 6 * tile : 6 * tile + 6] = part[:, 128 * tile : 128 * tile + 128].reshape(4, 2, 6, 16, 128)
        back_a.cross(q)

    each("middle", *back_b.first)
    back_a.add_cores()
    each("start", *back_a.first)
    each("finish", *back_b.first)
    each("start", *back_b.second)
    each("middle", *back_a.first)
    each("middle", *back_b.second)
    each("finish", *back_b.second)
    each("start", *back_b.third)
    each("finish", *back_a.first)
    each("start", *back_a.second)
    each("middle", *back_b.third)
    each("middle", *back_a.second)
    each("finish", *back_b.third)
    back_b.send_far()
    each("finish", *back_a.second)
    each("start", *back_a.third)
    each("middle", *back_a.third)
    back_b.send_full()
    each("finish", *back_a.third)
    back_a.send_far()
    back_b.wait_full()
    for tile in range(5):
        lanes = slice(tile * 128, (tile + 1) * 128)
        for row in range(ROW_TILES):
            high = min(SHARD, 16 * row + 16)
            conv_out[16 * row : high, lanes] = back_b.tile(7 * tile + row)[0 : high - 16 * row]
        skip_out[:, lanes] = back_b.tile(7 * tile + 6)[0:SKIP]
    back_a.send_full()
    back_a.wait_full()
    for tile in range(3):
        wide = min(C0 - tile * 128, 128)
        for row in range(ROW_TILES):
            high = min(SHARD, 16 * row + 16)
            values = back_a.tile(6 * tile + row)[0 : high - 16 * row, 0:wide]
            down_out[16 * row : high, tile * 128 : tile * 128 + wide] = values

    for copy in copies.started:
        copy.wait_send()


def vmem(*shape):
    return pltpu.VMEM(shape, BF)


def tiles(*shape):
    return vmem(*shape, 16, 128)


def body(images, w_down, w_conv, w_skip, act_grad, short_grad):
    picture = images.reshape(512, C0)
    act_cot = act_grad.reshape(CELLS, C1)
    short_cot = short_grad.reshape(CELLS, C1)
    a, b = TILES_A.slots, TILES_B.slots
    slots = [tiles(3, *shape) for cut in (TILES_A, TILES_B) for pair in scatter_slots(cut) for shape in pair]

    outs = pl.pallas_call(
        kernel,
        out_shape=(
            jax.ShapeDtypeStruct((CELLS, C1), BF),
            jax.ShapeDtypeStruct((CELLS, C1), BF),
            jax.ShapeDtypeStruct((SHARD, C0), F32),
            jax.ShapeDtypeStruct((SHARD, C1), F32),
            jax.ShapeDtypeStruct((SKIP, C1), F32),
        ),
        in_specs=[pl.BlockSpec(memory_space=pltpu.VMEM)] * 6,
        out_specs=tuple([pl.BlockSpec(memory_space=pltpu.VMEM)] * 5),
        scratch_shapes=[
            tiles(4, 4, 2, a),
            tiles(4, 4, 2, b),
            tiles(4, 4, 2, a),
            tiles(4, 4, 2, b),
            tiles(4, 4, a),
            tiles(4, 4, b),
            tiles(4, 4, a),
            tiles(4, 4, b),
            tiles(TILES_A.own),
            tiles(TILES_B.own),
            tiles(TILES_A.own),
            tiles(TILES_B.own),
            tiles(4, TILES_A.own),
            tiles(4, TILES_B.own),
            vmem(len(PAIRS), LANES0, TILE),
            vmem(512, LANES0),
            vmem(9, CELLS, LANES0),
            vmem(CELLS, COLS),
            vmem(CELLS, COLS),
            pltpu.SemaphoreType.DMA((SEMS,)),
            pltpu.SemaphoreType.DMA((SEMS,)),
            *slots,
        ],
        compiler_params=pltpu.CompilerParams(
            collective_id=0, has_side_effects=True, vmem_limit_bytes=56 * 1024 * 1024
        ),
    )(picture, w_down, w_conv, w_skip, act_cot, short_cot)
    activated, shortcut, down, conv, skip = outs
    return (
        activated.reshape(act_grad.shape),
        shortcut.reshape(short_grad.shape),
        down,
        conv,
        skip,
    )


def solution(mesh):
    cells = P(("rep", "fsdp"), None, None, None)
    rows = P("fsdp", None)
    return jax.shard_map(
        body,
        mesh=mesh,
        in_specs=(cells, rows, rows, rows, cells, cells),
        out_specs=(cells, cells, rows, rows, rows),
        check_vma=False,
    )
```

time: 94.7 us -> 110 us (1.16)
  Pallas kernels: 89.2 us -> 104 us
    pallas_call x1, Pallas kernels: 89.2 us -> 104 us  [body(): pl.pallas_call(kernel, out_shape=(jax.ShapeDtypeStruct((CELLS, C1), BF),...]
where the time goes in v2:
time: 110 us; the launch traced here: 109 us
  Pallas kernels  104 us (95%)
  local copies, waits for them, and re-layouts  4.38 us (4%)
    pallas_call x1, Pallas kernels, body(): pl.pallas_call(kernel, out_shape=(jax.ShapeDtypeStruct((CELLS, C1), BF),...  104 us
    unnamed x13, local copies, waits for them, and re-layouts  4.38 us

profile of v2, /device:TPU:8, one launch (start us, length us, event | category | flops | bytes accessed | tf_op | source)
XLA Modules:
  0.0 109.3 jit_solution(17994797214461738074)
XLA Ops:
  0.6 104.2 %shard_map.101 = (bf16[128,640]{1,0:T(8,128)(2,1)}, bf16[128,640]{1,0:T(8,128)(2,1)}, f32[90,320]{1,0:T(8,128)}, f32[90,640]{1,0:T(8,128)}, f32[10,640]{1,0:T(8,128)}) custom-call(bf16[512,320]{1,0:T(8,128)(2,1)} %bitcast.5, bf16[90,320]{1,0:T(8,128)(2,1)} %wd.1, bf16[90,640]{1,0:T(8,128)(2,1)} %wc.1, bf16[10,640]{1,0:T(8,128)(2,1)} %ws.1, ...), custom_call_target="tpu_custom_call" | custom-call | tf_op jit(solution)/shard_map/pallas_call | solution.py:614
  104.9 0.0 copy-start.1
  104.9 0.0 copy-start.2
  104.9 1.6 %copy.16 = bf16[1,8,16,640]{3,2,1,0:T(8,128)(2,1)} copy(bf16[1,8,16,640]{3,2,1,0:T(8,128)(2,1)} %bitcast.9) | data formatting | bytes 327680
  106.5 0.0 copy-done.1
  106.5 0.0 copy-start
  106.5 0.7 copy.17
  107.2 0.0 copy-done.2
  107.2 0.7 copy.18
  107.9 0.0 copy-done
  107.9 0.0 copy-start.3
  107.9 0.7 copy.19
  108.6 0.1 copy-done.3
  108.6 0.6 copy.20
Async XLA Ops:
  104.9 1.7 %copy-start.1 = (bf16[128,640]{1,0:T(8,128)(2,1)S(1)}, bf16[128,640]{1,0:T(8,128)(2,1)}, u32[]{:S(2)}) copy-start(bf16[128,640]{1,0:T(8,128)(2,1)} %get-tuple-element.11) | copy-start | bytes 491524
  104.9 2.3 %copy-start.2 = (f32[90,320]{1,0:T(8,128)S(1)}, f32[90,320]{1,0:T(8,128)}, u32[]{:S(2)}) copy-start(f32[90,320]{1,0:T(8,128)} %get-tuple-element.22) | copy-start | bytes 345604
  106.5 1.3 %copy-start = (f32[90,640]{1,0:T(8,128)S(1)}, f32[90,640]{1,0:T(8,128)}, u32[]{:S(2)}) copy-start(f32[90,640]{1,0:T(8,128)} %get-tuple-element.23) | copy-start | bytes 691204
  107.9 0.8 copy-start.3

commit v3 on v2

v3 whole, which is shorter than its diff:
```python
import jax
import jax.numpy as jnp
from jax import lax
from jax.experimental import pallas as pl
from jax.experimental.pallas import tpu as pltpu
from jax.sharding import PartitionSpec as P

MESH = pl.DeviceIdType.MESH
BF = jnp.bfloat16
F32 = jnp.float32

C0, C1 = 320, 640
LANES0 = 384
SHARD = 90
PAD = 96
SKIP, SKIP_PAD = 10, 16
ROW_TILES = PAD // 16
CELLS = 128
TILE = 256
COLS = 32 * PAD
CHUNK = 8 * PAD
SEMS = 240
EPS = 1e-5


def source_of(col):
    shard, place = divmod(col, PAD)
    return SHARD * shard + place if place < SHARD else -1


def tile_taps():
    pairs = []
    for tile in range(COLS // TILE):
        cols = [source_of(c) for c in range(tile * TILE, (tile + 1) * TILE)]
        for tap in sorted({s // C0 for s in cols if s >= 0}):
            pairs.append((tile, tap))
    return pairs


PAIRS = tile_taps()


def iota(shape, axis):
    return lax.broadcasted_iota(jnp.int32, shape, axis)


def ones_where(mask):
    return jnp.where(mask, 1.0, 0.0).astype(BF)


def spread_matrix(tile, tap):
    lane = iota((1, TILE), 1) + tile * TILE
    shard = jnp.full((1, TILE), tile * TILE // PAD, jnp.int32)
    for edge in range(PAD, COLS, PAD):
        if tile * TILE < edge < (tile + 1) * TILE:
            shard = shard + jnp.where(lane >= edge, 1, 0)
    place = lane - PAD * shard
    channel = lane - (PAD - SHARD) * shard - C0 * tap
    good = (place < SHARD) & (channel >= 0) & (channel < C0)
    channel = jnp.where(good, channel, -1)
    return ones_where(iota((LANES0, TILE), 0) == channel)


def skip_matrix():
    lane = iota((1, 32 * SKIP_PAD), 1)
    shard = lane >> 4
    place = lane - SKIP_PAD * shard
    channel = jnp.where(place < SKIP, SKIP * shard + place, -1)
    return ones_where(iota((LANES0, 32 * SKIP_PAD), 0) == channel)


def shift_down(tap):
    kh, kw = divmod(tap, 3)
    cell = iota((CELLS, 1), 0)
    row, col = 2 * (cell >> 4) + kh - 1, 2 * (cell & 15) + kw - 1
    index = jnp.where((row >= 0) & (col >= 0), row * 32 + col, -1)
    return ones_where(iota((CELLS, 512), 1) == index)


def shift_conv(tap):
    kh, kw = divmod(tap, 3)
    cell = iota((CELLS, 1), 0)
    row, col = (cell >> 4) + kh - 1, (cell & 15) + kw - 1
    good = (row >= 0) & (row < 8) & (col >= 0) & (col < 16)
    index = jnp.where(good, row * 16 + col, -1)
    return ones_where(iota((CELLS, CELLS), 1) == index)


def dot(a, b):
    return lax.dot_general(a, b, (((1,), (0,)), ((), ())), preferred_element_type=F32)


def dot_nt(a, b):
    return lax.dot_general(a, b, (((1,), (1,)), ((), ())), preferred_element_type=F32)


def dot_tn(a, b):
    return lax.dot_general(a, b, (((0,), (0,)), ((), ())), preferred_element_type=F32)


def group_matrix(width, group_of):
    return ones_where(group_of(iota((width, width), 0)) == group_of(iota((width, width), 1)))


def group10(c):
    return (c * 6554) >> 16


def group20(c):
    return (c * 3277) >> 16


def group_sums(vectors, same):
    width = same.shape[0]
    row = iota((8, width), 0)
    stacked = jnp.zeros((8, width), F32)
    for number, vector in enumerate(vectors):
        rest = vector
        for term in range(3):
            part = rest.astype(BF).astype(F32)
            rest = rest - part
            stacked = jnp.where(row == 4 * number + term, part, stacked)
    sums = dot(stacked.astype(BF), same)
    return [jnp.sum(sums[4 * n : 4 * n + 4], axis=0, keepdims=True) for n in range(len(vectors))]


def normalise(values, same, count):
    (total,) = group_sums([jnp.sum(values, axis=0, keepdims=True)], same)
    centred = values - total * (1.0 / count)
    (square,) = group_sums([jnp.sum(centred * centred, axis=0, keepdims=True)], same)
    scale = lax.rsqrt(square * (1.0 / count) + EPS)
    return centred * scale, scale


def normalise_back(cotangent, normed, scale, same, count):
    sig = 1.0 / (1.0 + jnp.exp(-normed))
    slope = cotangent * (sig * (1.0 + normed * (1.0 - sig)))
    first, second = group_sums(
        [jnp.sum(slope, axis=0, keepdims=True), jnp.sum(slope * normed, axis=0, keepdims=True)], same
    )
    return scale * (slope - first * (1.0 / count) - normed * (second * (1.0 / count)))


def silu(normed):
    return normed / (1.0 + jnp.exp(-normed))


class Tiles:
    def __init__(self, count, slots):
        first = (count + 1) // 2
        self.routes = ((0, first), (first, count - first))
        self.slots, self.quarter = slots, slots // 4


TILES_A = Tiles(18, 20)
TILES_B = Tiles(35, 36)


class Copies:
    def __init__(self, send, recv):
        self.send, self.recv, self.started = send, recv, []

    def start(self, src, dst, device):
        number = len(self.started)
        copy = pltpu.make_async_remote_copy(
            src_ref=src,
            dst_ref=dst,
            send_sem=self.send.at[number],
            recv_sem=self.recv.at[number],
            device_id=device,
            device_id_type=MESH,
        )
        copy.start()
        self.started.append(copy)
        return copy


class Spread:
    def __init__(self, copies, piece, row, light, heavy, sibling):
        self.copies, self.piece, self.row, self.sibling = copies, piece, row, sibling
        self.light, self.heavy = light, heavy
        self.to = {}
        self.shared = []

    def send(self, i, j, device, name):
        ref = self.piece(i, j)
        self.to[name] = self.copies.start(ref, ref, device)

    def wait(self, *names):
        for name in names:
            self.to[name].wait_recv()

    def both(self, i):
        self.send(i, 0, self.heavy[0], ("after", i))
        self.send(i, 0, self.heavy[1], ("before", i))

    def s0(self):
        for d in (2, 1, 3):
            self.send(0, 0, self.light[d - 1], ("light", d))
        self.both(0)

    def s1(self):
        for d in (1, 3, 2):
            self.wait(("light", d))
            self.both(4 - d)

    def s2(self):
        self.wait(("after", 0))
        self.send(0, 3, self.heavy[0], ("far", 0))

    def s4(self):
        for i in (3, 1):
            self.wait(("before", i))
            self.send(i, 1, self.heavy[1], ("far", i))

    def s5(self):
        self.wait(("after", 2))
        self.send(2, 3, self.heavy[0], ("far", 2))
        self.wait(("after", 1), ("after", 3), ("before", 0), ("before", 2))

    def s6(self):
        self.wait(("far", 0), ("far", 1), ("far", 2), ("far", 3))

    def share(self, *offsets):
        for offset in offsets:
            ref = self.row(offset)
            self.shared.append(self.copies.start(ref, ref, self.sibling))

    def end(self):
        for copy in self.shared:
            copy.wait_recv()


def add_into(ref, *others):
    total = ref[...].astype(F32)
    for other in others:
        total = total + other[...].astype(F32)
    ref[...] = total.astype(BF)


class Collect:
    def __init__(self, copies, piece, light, heavy, lands, ends):
        self.copies, self.piece = copies, piece
        self.light, self.heavy = light, heavy
        self.lands, self.ends = lands, ends
        self.to = {}

    def send(self, i, j, land, device, name):
        self.to[name] = self.copies.start(self.piece(i, j), land, device)

    def r0(self):
        after, before = self.heavy
        for i, device in ((2, after), (1, before), (3, before), (0, after)):
            self.send(i, 2, self.lands.at[i], device, ("far", i))
        for i, j, device in ((2, 3, before), (1, 1, after), (3, 1, after), (0, 3, before)):
            self.send(i, j, self.lands.at[4 + i], device, ("near", i))

    def r1(self):
        after, before = self.heavy
        for i, j, device in ((2, 1, after), (1, 3, before), (3, 3, before), (0, 1, after)):
            self.to["far", i].wait_recv()
            add_into(self.piece(i, j), self.lands.at[i])
            self.send(i, j, self.lands.at[8 + i], device, ("next", i))

    def r2(self):
        for i in (2, 1, 3, 0):
            self.to["near", i].wait_recv()
            self.to["next", i].wait_recv()
            add_into(self.piece(i, 0), self.lands.at[4 + i], self.lands.at[8 + i])
            if i > 0:
                self.send(i, 0, self.ends.at[i - 1], self.light[i - 1], ("light", i))

    def r3(self):
        for i in (2, 1, 3):
            self.to["light", i].wait_recv()
        add_into(self.piece(0, 0), *(self.ends.at[slot] for slot in range(3)))


def each(method, *routes, args=()):
    for route in routes:
        getattr(route, method)(*args)


def pieces(buf, cut, at, tail):
    _, y, zl, _ = at
    one, two = (pl.ds(*route) for route in cut.routes)

    def piece0(i, j):
        return buf.at[((y + j) % 4, (zl + i) % 4, *tail, one)]

    def piece1(i, j):
        return buf.at[((y + i) % 4, (zl + j) % 4, *tail, two)]

    def row0(j):
        return buf.at[((y + j) % 4, pl.ds(0, 4), *tail, one)]

    def row1(j):
        return buf.at[(pl.ds(0, 4), (zl + j) % 4, *tail, two)]

    return (piece0, row0), (piece1, row1)


def spreads(copies, buf, cut, at, rings, sibling):
    (y_all, y_ring), (z_all, z_ring) = rings
    (piece0, row0), (piece1, row1) = pieces(buf, cut, at, (at[3],))
    return (
        Spread(copies, piece0, row0, z_all, y_ring, sibling),
        Spread(copies, piece1, row1, y_all, z_ring, sibling),
    )


class Gradients:
    def __init__(self, copies, grads, lands, sums, slots, cut, at, rings, devices):
        self.copies, self.grads, self.lands, self.sums, self.cut, self.at = copies, grads, lands, sums, cut, at
        (y_all, y_ring), (z_all, z_ring) = rings
        land0, end0, land1, end1, self.from_x, self.own, self.far, self.full = slots
        self.sibling, self.z_far, self.x_others = devices
        self.crossed = []
        (piece0, _), (piece1, _) = pieces(sums, cut, at, ())
        self.routes = (
            Collect(copies, piece0, z_all, y_ring, land0, end0),
            Collect(copies, piece1, y_all, z_ring, land1, end1),
        )

    def cross(self, q):
        core = self.at[3]
        self.crossed.append(self.copies.start(self.grads.at[q, :, 1 - core], self.lands.at[q], self.sibling))

    def add_cores(self):
        core = self.at[3]
        for q in range(4):
            self.crossed[q].wait_recv()
            total = self.grads[q, :, core].astype(F32) + self.lands[q].astype(F32)
            self.sums[q] = total.astype(BF)

    def quarter(self, c):
        _, y, zl, _ = self.at
        return self.sums.at[y, zl, pl.ds(self.cut.quarter * (c % 4), self.cut.quarter)]

    def send_x(self):
        x = self.at[0]
        self.x_copies = [
            self.copies.start(self.quarter(x + d), self.from_x.at[d - 1], self.x_others[d - 1]) for d in (1, 2, 3)
        ]

    def send_far(self):
        for copy in self.x_copies:
            copy.wait_recv()
        total = self.quarter(self.at[0])[...].astype(F32)
        for slot in range(3):
            total = total + self.from_x[slot].astype(F32)
        self.own[...] = total.astype(BF)
        self.far_copy = self.copies.start(self.own, self.far, self.z_far)

    def send_full(self):
        x = self.at[0]
        self.far_copy.wait_recv()
        self.full[x] = (self.own[...].astype(F32) + self.far[...].astype(F32)).astype(BF)
        mine = self.full.at[x]
        self.full_copies = [self.copies.start(mine, mine, other) for other in self.x_others]

    def wait_full(self):
        for copy in self.full_copies:
            copy.wait_recv()

    def tile(self, number):
        return self.full[divmod(number, self.cut.quarter)].astype(F32) * (1.0 / 256)


def kernel(
    img_in, wd_in, wc_in, ws_in, ag_in, sg_in,
    act_hbm, short_hbm, down_out, conv_out, skip_out,
    img, wd, wc, ws, ag, sg, act_out, short_out, local,
    ga, gb, grad_a, grad_b, sib_a, sib_b, sum_a, sum_b,
    spread, padded_img, taps, cols_img, cols_first,
    send, recv, *slots,
):
    rep, shard = lax.axis_index("rep"), lax.axis_index("fsdp")
    x, y, zl, core = rep % 4, shard // 8, (shard // 2) % 4, shard % 2
    z = (rep // 4) * 4 + zl

    def device(x, y, z, core):
        return ((z // 4) * 4 + x, (y * 4 + z % 4) * 2 + core)

    sibling = device(x, y, z, 1 - core)
    x_others = [device((x + d) % 4, y, z, core) for d in (1, 2, 3)]
    y_all = [device(x, (y + d) % 4, z, core) for d in (1, 2, 3)]
    z_all = [device(x, y, (z + d) % 8, core) for d in (1, 2 + 4 * core, 7)]
    z_two_back = device(x, y, (z + 6 + 4 * core) % 8, core)
    z_far = device(x, y, (z + 4) % 8, core)
    at = (x, y, zl, core)
    rings = ((y_all, (y_all[0], y_all[2])), (z_all, (z_all[0], z_all[2])))

    barrier = pltpu.get_barrier_semaphore()
    greeted = [sibling, z_far, z_two_back] + x_others + y_all + z_all
    for other in greeted:
        pl.semaphore_signal(barrier, inc=1, device_id=other, device_id_type=MESH)
    loads = [
        pltpu.make_async_copy(src, dst, local.at[number])
        for number, (src, dst) in enumerate(
            ((wd_in, wd), (wc_in, wc), (ws_in, ws), (img_in, img), (ag_in, ag), (sg_in, sg))
        )
    ]
    for load in loads:
        load.start()
    for load in loads[:3]:
        load.wait()

    def place_shard(buf, values, lane_tile, per_lane, lanes):
        low = lane_tile * 128
        base = per_lane * lane_tile
        if lanes < 128:
            for row in range(ROW_TILES):
                buf[y, zl, core, base + row] = jnp.zeros((16, 128), BF)
            for row in range(ROW_TILES):
                high = min(SHARD, 16 * row + 16)
                buf[y, zl, core, base + row, 0 : high - 16 * row, 0:lanes] = values[16 * row : high, low : low + lanes]
        else:
            full = values[0:80, low : low + 128].reshape(5, 16, 128)
            buf[y, zl, core, base : base + 5] = full
            buf[y, zl, core, base + 5] = jnp.zeros((16, 128), BF)
            buf[y, zl, core, base + 5, 0:10] = values[80:SHARD, low : low + 128]

    for tile in range(3):
        place_shard(ga, wd, tile, 6, min(128, C0 - 128 * tile))
    for tile in range(5):
        place_shard(gb, wc, tile, 7, 128)
        gb[y, zl, core, 7 * tile + 6] = jnp.zeros((16, 128), BF)
        gb[y, zl, core, 7 * tile + 6, 0:SKIP] = ws[:, 128 * tile : 128 * tile + 128]

    pl.semaphore_wait(barrier, len(greeted))

    copies = Copies(send, recv)
    wa = spreads(copies, ga, TILES_A, at, rings, sibling)
    wb = spreads(copies, gb, TILES_B, at, rings, sibling)

    each("s0", *wa)
    each("s0", *wb)

    for number, (tile, tap) in enumerate(PAIRS):
        spread[number] = spread_matrix(tile, tap)
    for load in loads[3:]:
        load.wait()
    padded_img[...] = jnp.zeros((512, LANES0), BF)
    padded_img[:, 0:C0] = img[...]

    each("s1", *wa)
    each("s1", *wb)
    each("s2", *wa)
    each("share", *wa, args=(0,))
    each("s2", *wb)
    each("share", *wb, args=(0,))

    for tap in range(9):
        taps[tap] = dot(shift_down(tap), padded_img[...]).astype(BF)

    def columns(out):
        for tile in range(COLS // TILE):
            total = None
            for number, (tile_of, tap) in enumerate(PAIRS):
                if tile_of == tile:
                    term = dot(taps[tap], spread[number])
                    total = term if total is None else total + term
            out[:, tile * TILE : (tile + 1) * TILE] = total.astype(BF)

    each("s4", *wa)
    each("s5", *wa)
    each("share", *wa, args=(1, 3))
    each("s4", *wb)
    columns(cols_img)
    each("s6", *wa)
    each("share", *wa, args=(2,))
    each("s5", *wb)
    each("share", *wb, args=(1, 3))
    each("end", *wa)

    def chunk_of(q):
        return slice(q * CHUNK, (q + 1) * CHUNK)

    def rows_of(buf, q, lane_tiles, per_lane):
        parts = [
            buf[q, :, :, per_lane * tile : per_lane * tile + ROW_TILES].reshape(CHUNK, 128)
            for tile in range(lane_tiles)
        ]
        return jnp.concatenate(parts, axis=1)

    def down_rows(q):
        return rows_of(ga, q, 3, 6)

    def conv_rows(q):
        return rows_of(gb, q, 5, 7)

    reduced = sum(dot(cols_img[:, chunk_of(q)], down_rows(q)) for q in range(4)).astype(BF)
    same0 = group_matrix(LANES0, group10)
    normed0, scale0 = normalise(reduced.astype(F32), same0, CELLS * (C0 // 32))
    first = silu(normed0).astype(BF)
    for tap in range(9):
        taps[tap] = dot(shift_conv(tap), first).astype(BF)
    columns(cols_first)
    skip_spread = skip_matrix()
    reduced_cols = dot(reduced, skip_spread).astype(BF)
    grad_skip = dot_tn(reduced_cols, sg[...]).astype(BF)
    for tile in range(5):
        grad_b[:, :, :, 7 * tile + 6] = grad_skip[:, 128 * tile : 128 * tile + 128].reshape(4, 4, 2, 16, 128)
    grad_b[:, :, :, 35] = jnp.zeros((4, 4, 2, 16, 128), BF)
    grad_a[:, :, :, 18:20] = jnp.zeros((4, 4, 2, 2, 16, 128), BF)

    each("s6", *wb)
    each("share", *wb, args=(2,))
    each("end", *wb)

    hidden = sum(dot(cols_first[:, chunk_of(q)], conv_rows(q)) for q in range(4)).astype(BF)
    same1 = group_matrix(C1, group20)
    normed1, scale1 = normalise(hidden.astype(F32), same1, CELLS * (C1 // 32))
    act_out[...] = silu(normed1).astype(BF)
    act_store = pltpu.make_async_copy(act_out, act_hbm, local.at[6])
    act_store.start()
    d_hidden = normalise_back(ag[...].astype(F32), normed1, scale1, same1, CELLS * (C1 // 32)).astype(BF)

    devices = (sibling, z_far, x_others)
    back_a = Gradients(copies, grad_a, sib_a, sum_a, slots[:8], TILES_A, at, rings, devices)
    back_b = Gradients(copies, grad_b, sib_b, sum_b, slots[8:], TILES_B, at, rings, devices)

    for q in range(4):
        part = dot_tn(cols_first[:, chunk_of(q)], d_hidden).astype(BF)
        for tile in range(5):
            grad_b[q, :, :, 7 * tile : 7 * tile + 6] = part[:, 128 * tile : 128 * tile + 128].reshape(4, 2, 6, 16, 128)
        back_b.cross(q)

    for q in range(4):
        cols_first[:, chunk_of(q)] = dot_nt(d_hidden, conv_rows(q)).astype(BF)

    back_b.add_cores()
    each("r0", *back_b.routes)

    d_first = jnp.zeros((CELLS, LANES0), F32)
    for tap in range(9):
        part = None
        for number, (tile, tap_of) in enumerate(PAIRS):
            if tap_of == tap:
                term = dot_nt(cols_first[:, tile * TILE : (tile + 1) * TILE], spread[number])
                part = term if part is None else part + term
        d_first = d_first + dot(shift_conv(8 - tap), part.astype(BF))

    skip_rows = jnp.concatenate([gb[:, :, :, 7 * tile + 6].reshape(512, 128) for tile in range(5)], axis=1)
    short_out[...] = dot(reduced_cols, skip_rows).astype(BF)
    short_store = pltpu.make_async_copy(short_out, short_hbm, local.at[7])
    short_store.start()
    d_skip = dot_nt(dot_nt(sg[...], skip_rows).astype(BF), skip_spread)
    d_norm = normalise_back(
        d_first.astype(BF).astype(F32), normed0, scale0, same0, CELLS * (C0 // 32)
    )
    d_reduced = (d_norm + d_skip).astype(BF)

    for q in range(4):
        part = dot_tn(cols_img[:, chunk_of(q)], d_reduced).astype(BF)
        for tile in range(3):
            grad_a[q, :, :, 6 * tile : 6 * tile + 6] = part[:, 128 * tile : 128 * tile + 128].reshape(4, 2, 6, 16, 128)
        back_a.cross(q)

    each("r1", *back_b.routes)
    back_a.add_cores()
    each("r0", *back_a.routes)
    each("r2", *back_b.routes)
    each("r1", *back_a.routes)
    each("r3", *back_b.routes)
    back_b.send_x()
    each("r2", *back_a.routes)
    back_b.send_far()
    each("r3", *back_a.routes)
    back_a.send_x()
    back_b.send_full()
    back_a.send_far()
    back_b.wait_full()
    for tile in range(5):
        lanes = slice(tile * 128, (tile + 1) * 128)
        for row in range(ROW_TILES):
            high = min(SHARD, 16 * row + 16)
            conv_out[16 * row : high, lanes] = back_b.tile(7 * tile + row)[0 : high - 16 * row]
        skip_out[:, lanes] = back_b.tile(7 * tile + 6)[0:SKIP]
    back_a.send_full()
    back_a.wait_full()
    for tile in range(3):
        wide = min(C0 - tile * 128, 128)
        for row in range(ROW_TILES):
            high = min(SHARD, 16 * row + 16)
            values = back_a.tile(6 * tile + row)[0 : high - 16 * row, 0:wide]
            down_out[16 * row : high, tile * 128 : tile * 128 + wide] = values

    act_store.wait()
    short_store.wait()
    for copy in copies.started:
        copy.wait_send()


def vmem(*shape):
    return pltpu.VMEM(shape, BF)


def tiles(*shape):
    return vmem(*shape, 16, 128)


def body(images, w_down, w_conv, w_skip, act_grad, short_grad):
    picture = images.reshape(512, C0)
    act_cot = act_grad.reshape(CELLS, C1)
    short_cot = short_grad.reshape(CELLS, C1)
    a, b = TILES_A.slots, TILES_B.slots
    slots = []
    for cut in (TILES_A, TILES_B):
        for _, count in cut.routes:
            slots += [tiles(12, count), tiles(3, count)]
        slots += [tiles(3, cut.quarter), tiles(cut.quarter), tiles(cut.quarter), tiles(4, cut.quarter)]

    outs = pl.pallas_call(
        kernel,
        out_shape=(
            jax.ShapeDtypeStruct((CELLS, C1), BF),
            jax.ShapeDtypeStruct((CELLS, C1), BF),
            jax.ShapeDtypeStruct((SHARD, C0), F32),
            jax.ShapeDtypeStruct((SHARD, C1), F32),
            jax.ShapeDtypeStruct((SKIP, C1), F32),
        ),
        in_specs=[pl.BlockSpec(memory_space=pl.ANY)] * 6,
        out_specs=tuple([pl.BlockSpec(memory_space=pl.ANY)] * 2 + [pl.BlockSpec(memory_space=pltpu.VMEM)] * 3),
        scratch_shapes=[
            vmem(512, C0),
            vmem(SHARD, C0),
            vmem(SHARD, C1),
            vmem(SKIP, C1),
            *[vmem(CELLS, C1)] * 4,
            pltpu.SemaphoreType.DMA((8,)),
            tiles(4, 4, 2, a),
            tiles(4, 4, 2, b),
            tiles(4, 4, 2, a),
            tiles(4, 4, 2, b),
            tiles(4, 4, a),
            tiles(4, 4, b),
            tiles(4, 4, a),
            tiles(4, 4, b),
            vmem(len(PAIRS), LANES0, TILE),
            vmem(512, LANES0),
            vmem(9, CELLS, LANES0),
            vmem(CELLS, COLS),
            vmem(CELLS, COLS),
            pltpu.SemaphoreType.DMA((SEMS,)),
            pltpu.SemaphoreType.DMA((SEMS,)),
            *slots,
        ],
        compiler_params=pltpu.CompilerParams(
            collective_id=0, has_side_effects=True, vmem_limit_bytes=56 * 1024 * 1024
        ),
    )(picture, w_down, w_conv, w_skip, act_cot, short_cot)
    activated, shortcut, down, conv, skip = outs
    return (
        activated.reshape(act_grad.shape),
        shortcut.reshape(short_grad.shape),
        down,
        conv,
        skip,
    )


def solution(mesh):
    cells = P(("rep", "fsdp"), None, None, None)
    rows = P("fsdp", None)
    return jax.shard_map(
        body,
        mesh=mesh,
        in_specs=(cells, rows, rows, rows, cells, cells),
        out_specs=(cells, cells, rows, rows, rows),
        check_vma=False,
    )
```

time: 110 us -> 89.4 us (0.81)
  Pallas kernels: 104 us -> 83.6 us
    pallas_call x1, Pallas kernels: 104 us -> 83.6 us  [body(): pl.pallas_call(kernel, out_shape=(jax.ShapeDtypeStruct((CELLS, C1), BF),...]
where the time goes in v3:
time: 89.4 us; the launch traced here: 88.7 us
  Pallas kernels  83.6 us (94%)
  local copies, waits for them, and re-layouts  4.38 us (5%)
    pallas_call x1, Pallas kernels, body(): pl.pallas_call(kernel, out_shape=(jax.ShapeDtypeStruct((CELLS, C1), BF),...  83.6 us
    unnamed x13, local copies, waits for them, and re-layouts  4.38 us

profile of v3, /device:TPU:8, one launch (start us, length us, event | category | flops | bytes accessed | tf_op | source)
XLA Modules:
  0.0 88.7 jit_solution(12538723654309619671)
XLA Ops:
  0.6 83.6 %shard_map.101 = (bf16[128,640]{1,0:T(8,128)(2,1)}, bf16[128,640]{1,0:T(8,128)(2,1)}, f32[90,320]{1,0:T(8,128)}, f32[90,640]{1,0:T(8,128)}, f32[10,640]{1,0:T(8,128)}) custom-call(bf16[512,320]{1,0:T(8,128)(2,1)} %bitcast.5, bf16[90,320]{1,0:T(8,128)(2,1)} %wd_in.1, bf16[90,640]{1,0:T(8,128)(2,1)} %wc_in.1, bf16[10,640]{1,0:T(8,128)(2,1)} %ws_in.1, ...), custom_call_target="tpu_custom_call" | custom-call | tf_op jit(solution)/shard_map/pallas_call | solution.py:615
  84.3 0.0 copy-start.1
  84.3 0.0 copy-start.2
  84.3 1.6 %copy.16 = bf16[1,8,16,640]{3,2,1,0:T(8,128)(2,1)} copy(bf16[1,8,16,640]{3,2,1,0:T(8,128)(2,1)} %bitcast.9) | data formatting | bytes 327680
  85.9 0.0 copy-done.1
  85.9 0.0 copy-start
  85.9 0.7 copy.17
  86.6 0.0 copy-done.2
  86.6 0.7 copy.18
  87.3 0.0 copy-done
  87.3 0.0 copy-start.3
  87.3 0.7 copy.19
  88.0 0.1 copy-done.3
  88.1 0.6 copy.20
Async XLA Ops:
  84.3 1.7 %copy-start.1 = (bf16[128,640]{1,0:T(8,128)(2,1)S(1)}, bf16[128,640]{1,0:T(8,128)(2,1)}, u32[]{:S(2)}) copy-start(bf16[128,640]{1,0:T(8,128)(2,1)} %get-tuple-element.11) | copy-start | bytes 491524
  84.3 2.3 %copy-start.2 = (f32[90,320]{1,0:T(8,128)S(1)}, f32[90,320]{1,0:T(8,128)}, u32[]{:S(2)}) copy-start(f32[90,320]{1,0:T(8,128)} %get-tuple-element.22) | copy-start | bytes 345604
  85.9 1.3 %copy-start = (f32[90,640]{1,0:T(8,128)S(1)}, f32[90,640]{1,0:T(8,128)}, u32[]{:S(2)}) copy-start(f32[90,640]{1,0:T(8,128)} %get-tuple-element.23) | copy-start | bytes 691204
  87.3 0.8 copy-start.3

commit v4 on v3

--- a/solution.py
+++ b/solution.py
@@ -19,7 +19,7 @@
 TILE = 256
 COLS = 32 * PAD
 CHUNK = 8 * PAD
-SEMS = 240
+SEMS = 84
 EPS = 1e-5
 
 
@@ -157,78 +157,81 @@
 
 
 class Copies:
-    def __init__(self, send, recv):
-        self.send, self.recv, self.started = send, recv, []
-
-    def start(self, src, dst, device):
-        number = len(self.started)
-        copy = pltpu.make_async_remote_copy(
+    def __init__(self, sems):
+        self.sems, self.numbers = sems, {}
+
+    def sem(self, *key):
+        return self.sems.at[self.numbers.setdefault(key, len(self.numbers))]
+
+    def start(self, src, dst, device, send, recv):
+        pltpu.make_async_remote_copy(
             src_ref=src,
             dst_ref=dst,
-            send_sem=self.send.at[number],
-            recv_sem=self.recv.at[number],
+            send_sem=self.sem("send", *send),
+            recv_sem=self.sem("recv", *recv),
             device_id=device,
             device_id_type=MESH,
-        )
-        copy.start()
-        self.started.append(copy)
-        return copy
+        ).start()
+
+    def wait(self, way, key, ref):
+        pltpu.make_async_copy(ref, ref, self.sem(way, *key)).wait()
 
 
 class Spread:
-    def __init__(self, copies, piece, row, light, heavy, sibling):
-        self.copies, self.piece, self.row, self.sibling = copies, piece, row, sibling
-        self.light, self.heavy = light, heavy
-        self.to = {}
-        self.shared = []
-
-    def send(self, i, j, device, name):
+    def __init__(self, copies, name, piece, row, light, heavy, sibling, other, sent):
+        self.copies, self.name, self.piece, self.row, self.sibling = copies, name, piece, row, sibling
+        self.light, self.heavy, self.other, self.sent = light, heavy, other, sent
+
+    def send(self, i, j, device, recv):
         ref = self.piece(i, j)
-        self.to[name] = self.copies.start(ref, ref, device)
-
-    def wait(self, *names):
-        for name in names:
-            self.to[name].wait_recv()
+        self.copies.start(ref, ref, device, (self.name,), (self.name, recv))
+
+    def wait(self, recv, ref):
+        self.copies.wait("recv", (self.name, recv), ref)
 
     def both(self, i):
-        self.send(i, 0, self.heavy[0], ("after", i))
-        self.send(i, 0, self.heavy[1], ("before", i))
+        after, before = {0: ("a0", "rest"), 1: ("rest", "b"), 2: ("a2", "rest"), 3: ("rest", "b")}[i]
+        self.send(i, 0, self.heavy[0], after)
+        self.send(i, 0, self.heavy[1], before)
 
     def s0(self):
         for d in (2, 1, 3):
-            self.send(0, 0, self.light[d - 1], ("light", d))
+            self.send(0, 0, self.light[d - 1], d)
         self.both(0)
 
     def s1(self):
         for d in (1, 3, 2):
-            self.wait(("light", d))
+            self.wait(d, self.piece(4 - d, 0))
             self.both(4 - d)
 
     def s2(self):
-        self.wait(("after", 0))
-        self.send(0, 3, self.heavy[0], ("far", 0))
+        self.wait("a0", self.piece(0, 3))
+        self.send(0, 3, self.heavy[0], "far")
 
     def s4(self):
+        self.wait("b", self.sent.at[pl.ds(0, 2)])
         for i in (3, 1):
-            self.wait(("before", i))
-            self.send(i, 1, self.heavy[1], ("far", i))
+            self.send(i, 1, self.heavy[1], "far")
 
     def s5(self):
-        self.wait(("after", 2))
-        self.send(2, 3, self.heavy[0], ("far", 2))
-        self.wait(("after", 1), ("after", 3), ("before", 0), ("before", 2))
+        self.wait("a2", self.piece(2, 3))
+        self.send(2, 3, self.heavy[0], "far")
+        self.wait("rest", self.sent.at[pl.ds(0, 4)])
 
     def s6(self):
-        self.wait(("far", 0), ("far", 1), ("far", 2), ("far", 3))
+        self.wait("far", self.row(2))
 
     def share(self, *offsets):
         for offset in offsets:
             ref = self.row(offset)
-            self.shared.append(self.copies.start(ref, ref, self.sibling))
+            self.copies.start(ref, ref, self.sibling, (self.name, "core"), (self.name, "core"))
 
     def end(self):
-        for copy in self.shared:
-            copy.wait_recv()
+        self.copies.wait("recv", (self.name, "core"), self.other)
+
+    def drain(self):
+        self.copies.wait("send", (self.name, "core"), self.other)
+        self.copies.wait("send", (self.name,), self.sent)
 
 
 def add_into(ref, *others):
@@ -239,41 +242,46 @@
 
 
 class Collect:
-    def __init__(self, copies, piece, light, heavy, lands, ends):
-        self.copies, self.piece = copies, piece
-        self.light, self.heavy = light, heavy
-        self.lands, self.ends = lands, ends
-        self.to = {}
-
-    def send(self, i, j, land, device, name):
-        self.to[name] = self.copies.start(self.piece(i, j), land, device)
+    def __init__(self, copies, name, piece, light, heavy, lands):
+        self.copies, self.name, self.piece = copies, name, piece
+        self.light, self.heavy, self.lands = light, heavy, lands
+
+    def send(self, i, j, land, device, recv):
+        self.copies.start(self.piece(i, j), self.lands.at[land], device, (self.name,), (self.name, recv))
+
+    def wait(self, recv, start, count):
+        self.copies.wait("recv", (self.name, recv), self.lands.at[pl.ds(start, count)])
 
     def r0(self):
         after, before = self.heavy
-        for i, device in ((2, after), (1, before), (3, before), (0, after)):
-            self.send(i, 2, self.lands.at[i], device, ("far", i))
+        for slot, (i, device) in enumerate(((2, after), (1, before), (3, before), (0, after))):
+            self.send(i, 2, slot, device, ("far", slot // 2))
         for i, j, device in ((2, 3, before), (1, 1, after), (3, 1, after), (0, 3, before)):
-            self.send(i, j, self.lands.at[4 + i], device, ("near", i))
+            self.send(i, j, 8 + i, device, "near")
 
     def r1(self):
         after, before = self.heavy
-        for i, j, device in ((2, 1, after), (1, 3, before), (3, 3, before), (0, 1, after)):
-            self.to["far", i].wait_recv()
-            add_into(self.piece(i, j), self.lands.at[i])
-            self.send(i, j, self.lands.at[8 + i], device, ("next", i))
+        for slot, (i, j, device) in enumerate(((2, 1, after), (1, 3, before), (3, 3, before), (0, 1, after))):
+            if slot % 2 == 0:
+                self.wait(("far", slot // 2), slot, 2)
+            add_into(self.piece(i, j), self.lands.at[slot])
+            self.send(i, j, 4 + slot, device, ("next", slot // 2))
 
     def r2(self):
-        for i in (2, 1, 3, 0):
-            self.to["near", i].wait_recv()
-            self.to["next", i].wait_recv()
-            add_into(self.piece(i, 0), self.lands.at[4 + i], self.lands.at[8 + i])
+        self.wait("near", 8, 4)
+        for slot, i in enumerate((2, 1, 3, 0)):
+            if slot % 2 == 0:
+                self.wait(("next", slot // 2), 4 + slot, 2)
+            add_into(self.piece(i, 0), self.lands.at[8 + i], self.lands.at[4 + slot])
             if i > 0:
-                self.send(i, 0, self.ends.at[i - 1], self.light[i - 1], ("light", i))
+                self.send(i, 0, 11 + i, self.light[i - 1], "light")
 
     def r3(self):
-        for i in (2, 1, 3):
-            self.to["light", i].wait_recv()
-        add_into(self.piece(0, 0), *(self.ends.at[slot] for slot in range(3)))
+        self.wait("light", 12, 3)
+        add_into(self.piece(0, 0), *(self.lands.at[slot] for slot in (12, 13, 14)))
+
+    def drain(self):
+        self.copies.wait("send", (self.name,), self.lands)
 
 
 def each(method, *routes, args=()):
@@ -300,36 +308,37 @@
     return (piece0, row0), (piece1, row1)
 
 
-def spreads(copies, buf, cut, at, rings, sibling):
+def spreads(copies, name, buf, cut, at, rings, sibling, lands):
     (y_all, y_ring), (z_all, z_ring) = rings
     (piece0, row0), (piece1, row1) = pieces(buf, cut, at, (at[3],))
+    other0, other1 = (buf.at[pl.ds(0, 4), pl.ds(0, 4), 1 - at[3], pl.ds(*route)] for route in cut.routes)
     return (
-        Spread(copies, piece0, row0, z_all, y_ring, sibling),
-        Spread(copies, piece1, row1, y_all, z_ring, sibling),
+        Spread(copies, (name, 0), piece0, row0, z_all, y_ring, sibling, other0, lands[0]),
+        Spread(copies, (name, 1), piece1, row1, y_all, z_ring, sibling, other1, lands[1]),
     )
 
 
 class Gradients:
-    def __init__(self, copies, grads, lands, sums, slots, cut, at, rings, devices):
+    def __init__(self, copies, name, grads, lands, sums, slots, cut, at, rings, devices):
         self.copies, self.grads, self.lands, self.sums, self.cut, self.at = copies, grads, lands, sums, cut, at
         (y_all, y_ring), (z_all, z_ring) = rings
-        land0, end0, land1, end1, self.from_x, self.own, self.far, self.full = slots
+        land0, land1, self.ends, self.full = slots
         self.sibling, self.z_far, self.x_others = devices
-        self.crossed = []
+        self.name = name
         (piece0, _), (piece1, _) = pieces(sums, cut, at, ())
         self.routes = (
-            Collect(copies, piece0, z_all, y_ring, land0, end0),
-            Collect(copies, piece1, y_all, z_ring, land1, end1),
+            Collect(copies, (name, 2), piece0, z_all, y_ring, land0),
+            Collect(copies, (name, 3), piece1, y_all, z_ring, land1),
         )
 
     def cross(self, q):
-        core = self.at[3]
-        self.crossed.append(self.copies.start(self.grads.at[q, :, 1 - core], self.lands.at[q], self.sibling))
+        core, key = self.at[3], (self.name, "cross")
+        self.copies.start(self.grads.at[q, :, 1 - core], self.lands.at[q], self.sibling, key, key)
 
     def add_cores(self):
         core = self.at[3]
+        self.copies.wait("recv", (self.name, "cross"), self.lands)
         for q in range(4):
-            self.crossed[q].wait_recv()
             total = self.grads[q, :, core].astype(F32) + self.lands[q].astype(F32)
             self.sums[q] = total.astype(BF)
 
@@ -339,41 +348,42 @@
 
     def send_x(self):
         x = self.at[0]
-        self.x_copies = [
-            self.copies.start(self.quarter(x + d), self.from_x.at[d - 1], self.x_others[d - 1]) for d in (1, 2, 3)
-        ]
+        for d in (1, 2, 3):
+            self.copies.start(
+                self.quarter(x + d), self.ends.at[d - 1], self.x_others[d - 1], (self.name,), (self.name, "x")
+            )
 
     def send_far(self):
-        for copy in self.x_copies:
-            copy.wait_recv()
+        self.copies.wait("recv", (self.name, "x"), self.ends.at[pl.ds(0, 3)])
         total = self.quarter(self.at[0])[...].astype(F32)
         for slot in range(3):
-            total = total + self.from_x[slot].astype(F32)
-        self.own[...] = total.astype(BF)
-        self.far_copy = self.copies.start(self.own, self.far, self.z_far)
+            total = total + self.ends[slot].astype(F32)
+        self.ends[3] = total.astype(BF)
+        self.copies.start(self.ends.at[3], self.ends.at[4], self.z_far, (self.name,), (self.name, "z"))
 
     def send_full(self):
         x = self.at[0]
-        self.far_copy.wait_recv()
-        self.full[x] = (self.own[...].astype(F32) + self.far[...].astype(F32)).astype(BF)
+        self.copies.wait("recv", (self.name, "z"), self.ends.at[4])
+        self.full[x] = (self.ends[3].astype(F32) + self.ends[4].astype(F32)).astype(BF)
         mine = self.full.at[x]
-        self.full_copies = [self.copies.start(mine, mine, other) for other in self.x_others]
+        for other in self.x_others:
+            self.copies.start(mine, mine, other, (self.name,), (self.name, "full"))
 
     def wait_full(self):
-        for copy in self.full_copies:
-            copy.wait_recv()
-
-    def tile(self, number):
-        return self.full[divmod(number, self.cut.quarter)].astype(F32) * (1.0 / 256)
+        self.copies.wait("recv", (self.name, "full"), self.ends.at[pl.ds(0, 3)])
+
+    def drain(self):
+        self.copies.wait("send", (self.name, "cross"), self.lands)
+        self.copies.wait("send", (self.name,), self.ends)
 
 
 def kernel(
     img_in, wd_in, wc_in, ws_in, ag_in, sg_in,
-    act_hbm, short_hbm, down_out, conv_out, skip_out,
+    act_hbm, short_hbm, full_a_out, full_b_out,
     img, wd, wc, ws, ag, sg, act_out, short_out, local,
     ga, gb, grad_a, grad_b, sib_a, sib_b, sum_a, sum_b,
     spread, padded_img, taps, cols_img, cols_first,
-    send, recv, *slots,
+    sems, *slots,
 ):
     rep, shard = lax.axis_index("rep"), lax.axis_index("fsdp")
     x, y, zl, core = rep % 4, shard // 8, (shard // 2) % 4, shard % 2
@@ -430,9 +440,9 @@
 
     pl.semaphore_wait(barrier, len(greeted))
 
-    copies = Copies(send, recv)
-    wa = spreads(copies, ga, TILES_A, at, rings, sibling)
-    wb = spreads(copies, gb, TILES_B, at, rings, sibling)
+    copies = Copies(sems)
+    wa = spreads(copies, "a", ga, TILES_A, at, rings, sibling, slots[0:2])
+    wb = spreads(copies, "b", gb, TILES_B, at, rings, sibling, slots[4:6])
 
     each("s0", *wa)
     each("s0", *wb)
@@ -518,8 +528,8 @@
     d_hidden = normalise_back(ag[...].astype(F32), normed1, scale1, same1, CELLS * (C1 // 32)).astype(BF)
 
     devices = (sibling, z_far, x_others)
-    back_a = Gradients(copies, grad_a, sib_a, sum_a, slots[:8], TILES_A, at, rings, devices)
-    back_b = Gradients(copies, grad_b, sib_b, sum_b, slots[8:], TILES_B, at, rings, devices)
+    back_a = Gradients(copies, "a", grad_a, sib_a, sum_a, slots[:4], TILES_A, at, rings, devices)
+    back_b = Gradients(copies, "b", grad_b, sib_b, sum_b, slots[4:], TILES_B, at, rings, devices)
 
     for q in range(4):
         part = dot_tn(cols_first[:, chunk_of(q)], d_hidden).astype(BF)
@@ -572,25 +582,36 @@
     back_b.send_full()
     back_a.send_far()
     back_b.wait_full()
+    full_b_out[...] = back_b.full[...]
+    back_a.send_full()
+    back_a.wait_full()
+    full_a_out[...] = back_a.full[...]
+    act_store.wait()
+    short_store.wait()
+    assert len(copies.numbers) == SEMS
+    each("drain", *wa, *wb, *back_a.routes, *back_b.routes, back_a, back_b)
+
+
+def finish(act_in, short_in, full_a, full_b, act_out, short_out, down_out, conv_out, skip_out):
+    act_out[...] = act_in[...]
+    short_out[...] = short_in[...]
+
+    def rows(full, cut, number, high):
+        place = divmod(number, cut.quarter)
+        return full[place].astype(F32)[0:high] * (1.0 / 256)
+
     for tile in range(5):
         lanes = slice(tile * 128, (tile + 1) * 128)
         for row in range(ROW_TILES):
-            high = min(SHARD, 16 * row + 16)
-            conv_out[16 * row : high, lanes] = back_b.tile(7 * tile + row)[0 : high - 16 * row]
-        skip_out[:, lanes] = back_b.tile(7 * tile + 6)[0:SKIP]
-    back_a.send_full()
-    back_a.wait_full()
+            high = min(SHARD - 16 * row, 16)
+            conv_out[16 * row : 16 * row + high, lanes] = rows(full_b, TILES_B, 7 * tile + row, high)
+        skip_out[:, lanes] = rows(full_b, TILES_B, 7 * tile + 6, SKIP)
     for tile in range(3):
         wide = min(C0 - tile * 128, 128)
         for row in range(ROW_TILES):
-            high = min(SHARD, 16 * row + 16)
-            values = back_a.tile(6 * tile + row)[0 : high - 16 * row, 0:wide]
-            down_out[16 * row : high, tile * 128 : tile * 128 + wide] = values
-
-    act_store.wait()
-    short_store.wait()
-    for copy in copies.started:
-        copy.wait_send()
+            high = min(SHARD - 16 * row, 16)
+            values = rows(full_a, TILES_A, 6 * tile + row, high)
+            down_out[16 * row : 16 * row + high, tile * 128 : tile * 128 + wide] = values[:, 0:wide]
 
 
 def vmem(*shape):
@@ -609,20 +630,19 @@
     slots = []
     for cut in (TILES_A, TILES_B):
         for _, count in cut.routes:
-            slots += [tiles(12, count), tiles(3, count)]
-        slots += [tiles(3, cut.quarter), tiles(cut.quarter), tiles(cut.quarter), tiles(4, cut.quarter)]
+            slots.append(tiles(15, count))
+        slots += [tiles(7, cut.quarter), tiles(4, cut.quarter)]
 
     outs = pl.pallas_call(
         kernel,
         out_shape=(
             jax.ShapeDtypeStruct((CELLS, C1), BF),
             jax.ShapeDtypeStruct((CELLS, C1), BF),
-            jax.ShapeDtypeStruct((SHARD, C0), F32),
-            jax.ShapeDtypeStruct((SHARD, C1), F32),
-            jax.ShapeDtypeStruct((SKIP, C1), F32),
+            jax.ShapeDtypeStruct((4, TILES_A.quarter, 16, 128), BF),
+            jax.ShapeDtypeStruct((4, TILES_B.quarter, 16, 128), BF),
         ),
         in_specs=[pl.BlockSpec(memory_space=pl.ANY)] * 6,
-        out_specs=tuple([pl.BlockSpec(memory_space=pl.ANY)] * 2 + [pl.BlockSpec(memory_space=pltpu.VMEM)] * 3),
+        out_specs=tuple([pl.BlockSpec(memory_space=pl.ANY)] * 2 + [pl.BlockSpec(memory_space=pltpu.VMEM)] * 2),
         scratch_shapes=[
             vmem(512, C0),
             vmem(SHARD, C0),
@@ -644,14 +664,24 @@
             vmem(CELLS, COLS),
             vmem(CELLS, COLS),
             pltpu.SemaphoreType.DMA((SEMS,)),
-            pltpu.SemaphoreType.DMA((SEMS,)),
             *slots,
         ],
         compiler_params=pltpu.CompilerParams(
             collective_id=0, has_side_effects=True, vmem_limit_bytes=56 * 1024 * 1024
         ),
     )(picture, w_down, w_conv, w_skip, act_cot, short_cot)
-    activated, shortcut, down, conv, skip = outs
+    activated, shortcut, down, conv, skip = pl.pallas_call(
+        finish,
+        out_shape=(
+            jax.ShapeDtypeStruct((CELLS, C1), BF),
+            jax.ShapeDtypeStruct((CELLS, C1), BF),
+            jax.ShapeDtypeStruct((SHARD, C0), F32),
+            jax.ShapeDtypeStruct((SHARD, C1), F32),
+            jax.ShapeDtypeStruct((SKIP, C1), F32),
+        ),
+        in_specs=[pl.BlockSpec(memory_space=pltpu.VMEM)] * 4,
+        out_specs=tuple([pl.BlockSpec(memory_space=pltpu.VMEM)] * 5),
+    )(*outs)
     return (
         activated.reshape(act_grad.shape),
         shortcut.reshape(short_grad.shape),

time: 89.4 us -> 84 us (0.940)
  local copies, waits for them, and re-layouts: 4.38 us -> 0 us
  Pallas kernels: 83.6 us -> 82.7 us
    unnamed x13 -> x0, local copies, waits for them, and re-layouts: 4.38 us -> none
    pallas_call x1, Pallas kernels: 83.6 us -> 80.7 us  [body(): pl.pallas_call(kernel, out_shape=(jax.ShapeDtypeStruct((CELLS, C1), BF),...]
    pallas_call x0 -> x1, Pallas kernels: none -> 1.99 us  [body(): pl.pallas_call(finish, out_shape=(jax.ShapeDtypeStruct((CELLS, C1), BF),...]
where the time goes in v4:
time: 84 us; the launch traced here: 83.3 us
  Pallas kernels  82.7 us (98%)
    pallas_call x1, Pallas kernels, body(): pl.pallas_call(kernel, out_shape=(jax.ShapeDtypeStruct((CELLS, C1), BF),...  80.7 us
    pallas_call x1, Pallas kernels, body(): pl.pallas_call(finish, out_shape=(jax.ShapeDtypeStruct((CELLS, C1), BF),...  1.99 us

profile of v4, /device:TPU:8, one launch (start us, length us, event | category | flops | bytes accessed | tf_op | source)
XLA Modules:
  0.0 83.3 jit_solution(5223795425649552492)
XLA Ops:
  0.6 80.7 %shard_map.101 = (bf16[128,640]{1,0:T(8,128)(2,1)}, bf16[128,640]{1,0:T(8,128)(2,1)}, bf16[4,5,16,128]{3,2,1,0:T(8,128)(2,1)}, bf16[4,9,16,128]{3,2,1,0:T(8,128)(2,1)}) custom-call(bf16[512,320]{1,0:T(8,128)(2,1)} %bitcast.5, bf16[90,320]{1,0:T(8,128)(2,1)} %wd_in.1, bf16[90,640]{1,0:T(8,128)(2,1)} %wc_in.1, bf16[10,640]{1,0:T(8,128)(2,1)} %ws_in.1, ...), custom_call_target="tpu_custom_call" | custom-call | tf_op jit(solution)/shard_map/pallas_call | solution.py:636
  81.4 2.0 %shard_map.102 = (bf16[128,640]{1,0:T(8,128)(2,1)}, bf16[128,640]{1,0:T(8,128)(2,1)}, f32[90,320]{1,0:T(8,128)}, f32[90,640]{1,0:T(8,128)}, f32[10,640]{1,0:T(8,128)}) custom-call(bf16[128,640]{1,0:T(8,128)(2,1)} %get-tuple-element.14.act_in, bf16[128,640]{1,0:T(8,128)(2,1)} %get-tuple-element.15.short_in, bf16[4,5,16,128]{3,2,1,0:T(8,128)(2,1)} %get-tuple-element.16.full_a, ...), custom_call_target="tpu_custom_call" | custom-call | tf_op jit(solution)/shard_map/pallas_call | solution.py:673

commit v5 on v4

--- a/solution.py
+++ b/solution.py
@@ -19,7 +19,7 @@
 TILE = 256
 COLS = 32 * PAD
 CHUNK = 8 * PAD
-SEMS = 84
+SEMS = 92
 EPS = 1e-5
 
 
@@ -195,8 +195,10 @@
         self.send(i, 0, self.heavy[1], before)
 
     def s0(self):
-        for d in (2, 1, 3):
+        for d in (1, 3, 2):
             self.send(0, 0, self.light[d - 1], d)
+
+    def own(self):
         self.both(0)
 
     def s1(self):
@@ -211,15 +213,25 @@
     def s4(self):
         self.wait("b", self.sent.at[pl.ds(0, 2)])
         for i in (3, 1):
-            self.send(i, 1, self.heavy[1], "far")
+            self.send(i, 1, self.heavy[1], "far2")
 
     def s5(self):
         self.wait("a2", self.piece(2, 3))
-        self.send(2, 3, self.heavy[0], "far")
+        self.send(2, 3, self.heavy[0], "far3")
         self.wait("rest", self.sent.at[pl.ds(0, 4)])
 
+    def share_far(self, i):
+        ref = self.piece(i, 2)
+        self.copies.start(ref, ref, self.sibling, (self.name, "core"), (self.name, "core"))
+
     def s6(self):
-        self.wait("far", self.row(2))
+        self.wait("far", self.piece(0, 2))
+        self.share_far(0)
+        self.wait("far2", self.sent.at[pl.ds(0, 2)])
+        self.share_far(1)
+        self.share_far(3)
+        self.wait("far3", self.piece(2, 2))
+        self.share_far(2)
 
     def share(self, *offsets):
         for offset in offsets:
@@ -446,6 +458,8 @@
 
     each("s0", *wa)
     each("s0", *wb)
+    each("own", *wa)
+    each("own", *wb)
 
     for number, (tile, tap) in enumerate(PAIRS):
         spread[number] = spread_matrix(tile, tap)
@@ -479,7 +493,6 @@
     each("s4", *wb)
     columns(cols_img)
     each("s6", *wa)
-    each("share", *wa, args=(2,))
     each("s5", *wb)
     each("share", *wb, args=(1, 3))
     each("end", *wa)
@@ -516,7 +529,6 @@
     grad_a[:, :, :, 18:20] = jnp.zeros((4, 4, 2, 2, 16, 128), BF)
 
     each("s6", *wb)
-    each("share", *wb, args=(2,))
     each("end", *wb)
 
     hidden = sum(dot(cols_first[:, chunk_of(q)], conv_rows(q)) for q in range(4)).astype(BF)
@@ -539,9 +551,6 @@
 
     for q in range(4):
         cols_first[:, chunk_of(q)] = dot_nt(d_hidden, conv_rows(q)).astype(BF)
-
-    back_b.add_cores()
-    each("r0", *back_b.routes)
 
     d_first = jnp.zeros((CELLS, LANES0), F32)
     for tap in range(9):
@@ -557,6 +566,9 @@
     short_store = pltpu.make_async_copy(short_out, short_hbm, local.at[7])
     short_store.start()
     d_skip = dot_nt(dot_nt(sg[...], skip_rows).astype(BF), skip_spread)
+    back_b.add_cores()
+    each("r0", *back_b.routes)
+
     d_norm = normalise_back(
         d_first.astype(BF).astype(F32), normed0, scale0, same0, CELLS * (C0 // 32)
     )
@@ -579,8 +591,8 @@
     back_b.send_far()
     each("r3", *back_a.routes)
     back_a.send_x()
+    back_a.send_far()
     back_b.send_full()
-    back_a.send_far()
     back_b.wait_full()
     full_b_out[...] = back_b.full[...]
     back_a.send_full()

time: 84 us -> 82.5 us (0.982)
  Pallas kernels: 82.7 us -> 81.7 us
    pallas_call x1, Pallas kernels: 80.7 us -> 79.7 us  [body(): pl.pallas_call(kernel, out_shape=(jax.ShapeDtypeStruct((CELLS, C1), BF),...]
where the time goes in v5:
time: 82.5 us; the launch traced here: 82.3 us
  Pallas kernels  81.7 us (99%)
    pallas_call x1, Pallas kernels, body(): pl.pallas_call(kernel, out_shape=(jax.ShapeDtypeStruct((CELLS, C1), BF),...  79.7 us
    pallas_call x1, Pallas kernels, body(): pl.pallas_call(finish, out_shape=(jax.ShapeDtypeStruct((CELLS, C1), BF),...  1.99 us

profile of v5, /device:TPU:8, one launch (start us, length us, event | category | flops | bytes accessed | tf_op | source)
XLA Modules:
  0.0 82.3 jit_solution(3083532310106641517)
XLA Ops:
  0.6 79.7 %shard_map.101 = (bf16[128,640]{1,0:T(8,128)(2,1)}, bf16[128,640]{1,0:T(8,128)(2,1)}, bf16[4,5,16,128]{3,2,1,0:T(8,128)(2,1)}, bf16[4,9,16,128]{3,2,1,0:T(8,128)(2,1)}) custom-call(bf16[512,320]{1,0:T(8,128)(2,1)} %bitcast.5, bf16[90,320]{1,0:T(8,128)(2,1)} %wd_in.1, bf16[90,640]{1,0:T(8,128)(2,1)} %wc_in.1, bf16[10,640]{1,0:T(8,128)(2,1)} %ws_in.1, ...), custom_call_target="tpu_custom_call" | custom-call | tf_op jit(solution)/shard_map/pallas_call | solution.py:648
  80.4 2.0 %shard_map.102 = (bf16[128,640]{1,0:T(8,128)(2,1)}, bf16[128,640]{1,0:T(8,128)(2,1)}, f32[90,320]{1,0:T(8,128)}, f32[90,640]{1,0:T(8,128)}, f32[10,640]{1,0:T(8,128)}) custom-call(bf16[128,640]{1,0:T(8,128)(2,1)} %get-tuple-element.14.act_in, bf16[128,640]{1,0:T(8,128)(2,1)} %get-tuple-element.15.short_in, bf16[4,5,16,128]{3,2,1,0:T(8,128)(2,1)} %get-tuple-element.16.full_a, ...), custom_call_target="tpu_custom_call" | custom-call | tf_op jit(solution)/shard_map/pallas_call | solution.py:685

commit v6 on v5

--- a/solution.py
+++ b/solution.py
@@ -394,7 +394,7 @@
     act_hbm, short_hbm, full_a_out, full_b_out,
     img, wd, wc, ws, ag, sg, act_out, short_out, local,
     ga, gb, grad_a, grad_b, sib_a, sib_b, sum_a, sum_b,
-    spread, padded_img, taps, cols_img, cols_first,
+    spread, padded_img, taps, cols_img, cols_first, same0, same1, skip_spread,
     sems, *slots,
 ):
     rep, shard = lax.axis_index("rep"), lax.axis_index("fsdp")
@@ -463,6 +463,9 @@
 
     for number, (tile, tap) in enumerate(PAIRS):
         spread[number] = spread_matrix(tile, tap)
+    same0[...] = group_matrix(LANES0, group10)
+    same1[...] = group_matrix(C1, group20)
+    skip_spread[...] = skip_matrix()
     for load in loads[3:]:
         load.wait()
     padded_img[...] = jnp.zeros((512, LANES0), BF)
@@ -514,14 +517,12 @@
         return rows_of(gb, q, 5, 7)
 
     reduced = sum(dot(cols_img[:, chunk_of(q)], down_rows(q)) for q in range(4)).astype(BF)
-    same0 = group_matrix(LANES0, group10)
-    normed0, scale0 = normalise(reduced.astype(F32), same0, CELLS * (C0 // 32))
+    normed0, scale0 = normalise(reduced.astype(F32), same0[...], CELLS * (C0 // 32))
     first = silu(normed0).astype(BF)
     for tap in range(9):
         taps[tap] = dot(shift_conv(tap), first).astype(BF)
     columns(cols_first)
-    skip_spread = skip_matrix()
-    reduced_cols = dot(reduced, skip_spread).astype(BF)
+    reduced_cols = dot(reduced, skip_spread[...]).astype(BF)
     grad_skip = dot_tn(reduced_cols, sg[...]).astype(BF)
     for tile in range(5):
         grad_b[:, :, :, 7 * tile + 6] = grad_skip[:, 128 * tile : 128 * tile + 128].reshape(4, 4, 2, 16, 128)
@@ -532,12 +533,11 @@
     each("end", *wb)
 
     hidden = sum(dot(cols_first[:, chunk_of(q)], conv_rows(q)) for q in range(4)).astype(BF)
-    same1 = group_matrix(C1, group20)
-    normed1, scale1 = normalise(hidden.astype(F32), same1, CELLS * (C1 // 32))
+    normed1, scale1 = normalise(hidden.astype(F32), same1[...], CELLS * (C1 // 32))
     act_out[...] = silu(normed1).astype(BF)
     act_store = pltpu.make_async_copy(act_out, act_hbm, local.at[6])
     act_store.start()
-    d_hidden = normalise_back(ag[...].astype(F32), normed1, scale1, same1, CELLS * (C1 // 32)).astype(BF)
+    d_hidden = normalise_back(ag[...].astype(F32), normed1, scale1, same1[...], CELLS * (C1 // 32)).astype(BF)
 
     devices = (sibling, z_far, x_others)
     back_a = Gradients(copies, "a", grad_a, sib_a, sum_a, slots[:4], TILES_A, at, rings, devices)
@@ -565,12 +565,12 @@
     short_out[...] = dot(reduced_cols, skip_rows).astype(BF)
     short_store = pltpu.make_async_copy(short_out, short_hbm, local.at[7])
     short_store.start()
-    d_skip = dot_nt(dot_nt(sg[...], skip_rows).astype(BF), skip_spread)
+    d_skip = dot_nt(dot_nt(sg[...], skip_rows).astype(BF), skip_spread[...])
     back_b.add_cores()
     each("r0", *back_b.routes)
 
     d_norm = normalise_back(
-        d_first.astype(BF).astype(F32), normed0, scale0, same0, CELLS * (C0 // 32)
+        d_first.astype(BF).astype(F32), normed0, scale0, same0[...], CELLS * (C0 // 32)
     )
     d_reduced = (d_norm + d_skip).astype(BF)
 
@@ -675,6 +675,9 @@
             vmem(9, CELLS, LANES0),
             vmem(CELLS, COLS),
             vmem(CELLS, COLS),
+            vmem(LANES0, LANES0),
+            vmem(C1, C1),
+            vmem(LANES0, 32 * SKIP_PAD),
             pltpu.SemaphoreType.DMA((SEMS,)),
             *slots,
         ],

time: 82.5 us -> 82.1 us (level)
  no operation moved by 1% of the time
where the time goes in v6:
time: 82.1 us; the launch traced here: 82 us
  Pallas kernels  81.4 us (99%)
    pallas_call x1, Pallas kernels, body(): pl.pallas_call(kernel, out_shape=(jax.ShapeDtypeStruct((CELLS, C1), BF),...  79.4 us
    pallas_call x1, Pallas kernels, body(): pl.pallas_call(finish, out_shape=(jax.ShapeDtypeStruct((CELLS, C1), BF),...  1.99 us

profile of v6, /device:TPU:8, one launch (start us, length us, event | category | flops | bytes accessed | tf_op | source)
XLA Modules:
  0.0 82.0 jit_solution(15291741611418888501)
XLA Ops:
  0.6 79.4 %shard_map.101 = (bf16[128,640]{1,0:T(8,128)(2,1)}, bf16[128,640]{1,0:T(8,128)(2,1)}, bf16[4,5,16,128]{3,2,1,0:T(8,128)(2,1)}, bf16[4,9,16,128]{3,2,1,0:T(8,128)(2,1)}) custom-call(bf16[512,320]{1,0:T(8,128)(2,1)} %bitcast.5, bf16[90,320]{1,0:T(8,128)(2,1)} %wd_in.1, bf16[90,640]{1,0:T(8,128)(2,1)} %wc_in.1, bf16[10,640]{1,0:T(8,128)(2,1)} %ws_in.1, ...), custom_call_target="tpu_custom_call" | custom-call | tf_op jit(solution)/shard_map/pallas_call | solution.py:648
  80.0 2.0 %shard_map.102 = (bf16[128,640]{1,0:T(8,128)(2,1)}, bf16[128,640]{1,0:T(8,128)(2,1)}, f32[90,320]{1,0:T(8,128)}, f32[90,640]{1,0:T(8,128)}, f32[10,640]{1,0:T(8,128)}) custom-call(bf16[128,640]{1,0:T(8,128)(2,1)} %get-tuple-element.14.act_in, bf16[128,640]{1,0:T(8,128)(2,1)} %get-tuple-element.15.short_in, bf16[4,5,16,128]{3,2,1,0:T(8,128)(2,1)} %get-tuple-element.16.full_a, ...), custom_call_target="tpu_custom_call" | custom-call | tf_op jit(solution)/shard_map/pallas_call | solution.py:688
